TPU v7x, 512 devices: a whole 4x8x8 slice. The times are simulated.
512 devices in a mesh: ctx: 64 (over x, y_lo, z), tp: 8 (over y_hi, core).
Axes of the slice: x: 4, y: 8 (y_hi: 4, y_lo: 2; y = y_hi * 2 + y_lo), z: 8, core: 2. Of those that a mesh axis runs over, the one named last changes fastest.
Arguments:
- features: bfloat16 [8192, 4096], P('ctx'), may hold values from -6 to 6
- grad_out: bfloat16 [8192, 4096], P('ctx'), may hold values from -6 to 6
- w_value: bfloat16 [4096, 4096], P('ctx', 'tp'), may hold values from -0.09375 to 0.09375
- w_query: bfloat16 [4096, 4096], P('ctx', 'tp'), may hold values from -0.09375 to 0.09375
- w_out: bfloat16 [4096, 4096], P('tp', 'ctx'), may hold values from -0.09375 to 0.09375
- residues: float32 [16, 4096], P(None, 'tp'), may hold values from -0.3 to 0.3
- decays: float32 [16, 4096], P(None, 'tp'), may hold values from 3.0517578e-05 to 0.05
- freqs: float32 [16, 4096], P(None, 'tp'), may hold values from 0 to 0.2
- skips: float32 [4096], P('tp'), may hold values from 0.5 to 1.5
Outputs:
- mixed: bfloat16 [8192, 4096], P('ctx', 'tp')
- grad_in: bfloat16 [8192, 4096], P('ctx', 'tp')
- grad_residues: float32 [16, 4096], P(None, ('tp', 'ctx'))
All inputs are finite; a program needn't handle non-finite values.
Results may differ from a plain program's by a relative error of at most 0.023.
Values may be sent and summed in bfloat16 or wider, within the bound.
A program may use at most 128 MiB of HBM per device.

v0:
```python
from functools import partial
import math

import jax
import jax.numpy as jnp
from jax import lax
from jax.sharding import PartitionSpec as P

einsum_high = partial(jnp.einsum, precision=lax.Precision.HIGHEST)


def angle_table(rows, cols, period):
    left = jnp.arange(rows, dtype=jnp.int32)[:, None]
    right = jnp.arange(cols, dtype=jnp.int32)[None, :]
    phase = (left * right % period).astype(jnp.float32) * (-2.0 * math.pi / period)
    return (jnp.cos(phase), jnp.sin(phase))


def make_tables(outer, inner):
    first_cos, first_sin = angle_table(outer, outer, outer)
    twist_cos, twist_sin = angle_table(inner, outer, outer * inner)
    second_cos, second_sin = angle_table(inner, inner, inner)
    return (first_cos, first_sin, twist_cos, twist_sin, second_cos, second_sin)


def forward_dft(real, tables):
    first_cos, first_sin, twist_cos, twist_sin, second_cos, second_sin = tables
    step_re = einsum_high("Bab,af->Bbf", real, first_cos)
    step_im = einsum_high("Bab,af->Bbf", real, first_sin)
    turn_re = step_re * twist_cos - step_im * twist_sin
    turn_im = step_re * twist_sin + step_im * twist_cos
    spec_re = einsum_high("Bbf,bg->Bfg", turn_re, second_cos) - einsum_high(
        "Bbf,bg->Bfg", turn_im, second_sin
    )
    spec_im = einsum_high("Bbf,bg->Bfg", turn_re, second_sin) + einsum_high(
        "Bbf,bg->Bfg", turn_im, second_cos
    )
    return (spec_re, spec_im)


def inverse_dft(spec_re, spec_im, tables):
    first_cos, first_sin, twist_cos, twist_sin, second_cos, second_sin = tables
    turn_re = einsum_high("Bfg,bg->Bbf", spec_re, second_cos) + einsum_high(
        "Bfg,bg->Bbf", spec_im, second_sin
    )
    turn_im = einsum_high("Bfg,bg->Bbf", spec_im, second_cos) - einsum_high(
        "Bfg,bg->Bbf", spec_re, second_sin
    )
    step_re = turn_re * twist_cos + turn_im * twist_sin
    step_im = turn_im * twist_cos - turn_re * twist_sin
    real = einsum_high("Bbf,af->Bab", step_re, first_cos) + einsum_high(
        "Bbf,af->Bab", step_im, first_sin
    )
    total = first_cos.shape[0] * second_cos.shape[0]
    return real.reshape(real.shape[0], total) / total


def padded_spectrum(signal, outer, inner, tables):
    width = signal.shape[0]
    whole = jnp.concatenate([signal, jnp.zeros_like(signal)], axis=1).reshape(width, outer, inner)
    return forward_dft(whole, tables)


def times_conj(left_re, left_im, right_re, right_im):
    return (left_re * right_re + left_im * right_im, left_im * right_re - left_re * right_im)


def channel_spectra(value_chan, filt, outer, inner, tables):
    value_re, value_im = padded_spectrum(value_chan.astype(jnp.float32), outer, inner, tables)
    filt_re, filt_im = padded_spectrum(filt, outer, inner, tables)
    return (value_re, value_im, filt_re, filt_im)


def body(features, grad_out, w_value, w_query, w_out, residues, decays, freqs, skips):
    n_ctx = lax.axis_size("ctx")
    tok_rows = features.shape[0]
    seq_len = tok_rows * n_ctx
    group_width = w_value.shape[1]
    block_width = group_width // n_ctx
    outer = 2 * n_ctx
    tables = make_tables(outer, tok_rows)
    value_full = lax.all_gather(w_value, "ctx", axis=0, tiled=True)
    query_full = lax.all_gather(w_query, "ctx", axis=0, tiled=True)
    out_full = None
    contract_rows = (((0,), (1,)), ((), ()))
    value_t = lax.dot_general(
        value_full, features, contract_rows, preferred_element_type=jnp.float32
    ).astype(jnp.bfloat16)
    query_t = lax.dot_general(
        query_full, features, contract_rows, preferred_element_type=jnp.float32
    ).astype(jnp.bfloat16)
    value_chan = lax.all_to_all(value_t, "ctx", split_axis=0, concat_axis=1, tiled=True)
    first = lax.axis_index("ctx") * block_width
    res_blk = lax.dynamic_slice_in_dim(residues, first, block_width, 1)
    dec_blk = lax.dynamic_slice_in_dim(decays, first, block_width, 1)
    fre_blk = lax.dynamic_slice_in_dim(freqs, first, block_width, 1)
    skip_blk = lax.dynamic_slice_in_dim(skips, first, block_width, 0)
    positions = jnp.arange(seq_len).astype(jnp.float32)
    bases = []
    filt = jnp.zeros((block_width, seq_len), jnp.float32)
    for mode in range(residues.shape[0]):
        basis = jnp.exp(-dec_blk[mode][:, None] * positions[None, :]) * jnp.cos(
            fre_blk[mode][:, None] * positions[None, :]
        )
        bases.append(basis)
        filt = filt + res_blk[mode][:, None] * basis
    value_re, value_im, filt_re, filt_im = channel_spectra(
        value_chan, filt, outer, tok_rows, tables
    )
    prod_re = value_re * filt_re - value_im * filt_im
    prod_im = value_re * filt_im + value_im * filt_re
    conv = inverse_dft(prod_re, prod_im, tables)[:, :seq_len]
    state_chan = (conv + skip_blk[:, None] * value_chan.astype(jnp.float32)).astype(jnp.bfloat16)
    state_t = lax.all_to_all(state_chan, "ctx", split_axis=1, concat_axis=0, tiled=True)
    gated = (query_t.astype(jnp.float32) * state_t.astype(jnp.float32)).astype(jnp.bfloat16)
    out_full = lax.all_gather(w_out, "ctx", axis=1, tiled=True)
    mixed_t = lax.psum_scatter(
        lax.dot_general(
            out_full, gated, (((0,), (0,)), ((), ())), preferred_element_type=jnp.float32
        ).astype(jnp.bfloat16),
        "tp",
        scatter_dimension=0,
        tiled=True,
    ).astype(jnp.float32)
    mixed = mixed_t.T.astype(jnp.bfloat16)
    grad_gated = lax.dot_general(
        out_full, grad_out, (((1,), (1,)), ((), ())), preferred_element_type=jnp.float32
    )
    grad_query = (grad_gated * state_t.astype(jnp.float32)).astype(jnp.bfloat16)
    grad_state = (grad_gated * query_t.astype(jnp.float32)).astype(jnp.bfloat16)
    grad_chan = lax.all_to_all(grad_state, "ctx", split_axis=0, concat_axis=1, tiled=True)
    value_back = lax.all_to_all(value_t, "ctx", split_axis=0, concat_axis=1, tiled=True)
    value_re, value_im, filt_re, filt_im = channel_spectra(
        value_back, filt, outer, tok_rows, tables
    )
    grad_chan_f = grad_chan.astype(jnp.float32)
    grad_re, grad_im = padded_spectrum(grad_chan_f, outer, tok_rows, tables)
    back_re, back_im = times_conj(grad_re, grad_im, filt_re, filt_im)
    back = inverse_dft(back_re, back_im, tables)[:, :seq_len]
    grad_value_chan = (back + skip_blk[:, None] * grad_chan_f).astype(jnp.bfloat16)
    corr_re, corr_im = times_conj(grad_re, grad_im, value_re, value_im)
    grad_filt = inverse_dft(corr_re, corr_im, tables)[:, :seq_len]
    grad_residues = jnp.stack([jnp.sum(grad_filt * basis, axis=1) for basis in bases], axis=0)
    grad_value_t = lax.all_to_all(grad_value_chan, "ctx", split_axis=1, concat_axis=0, tiled=True)
    grad_in_t = lax.psum_scatter(
        (
            jnp.dot(query_full, grad_query, preferred_element_type=jnp.float32)
            + jnp.dot(value_full, grad_value_t, preferred_element_type=jnp.float32)
        ).astype(jnp.bfloat16),
        "tp",
        scatter_dimension=0,
        tiled=True,
    ).astype(jnp.float32)
    grad_in = grad_in_t.T.astype(jnp.bfloat16)
    return (mixed, grad_in, grad_residues)


def solution(mesh):
    placed = (
        P("ctx", None),
        P("ctx", None),
        P("ctx", "tp"),
        P("ctx", "tp"),
        P("tp", "ctx"),
        P(None, "tp"),
        P(None, "tp"),
        P(None, "tp"),
        P("tp"),
    )
    return jax.shard_map(
        body,
        mesh=mesh,
        in_specs=placed,
        out_specs=(P("ctx", "tp"), P("ctx", "tp"), P(None, ("tp", "ctx"))),
        check_vma=False,
    )
```

profile of v0, /device:TPU:1, one launch (start us, length us, event | category | flops | bytes accessed | tf_op | source)
XLA Modules:
  0.0 1105.5 jit_solution(8332260904114688633)
XLA Ops:
  9.4 1.3 dynamic_slice.15
  10.7 1.1 fusion.217
  11.9 1.2 fusion.214
  13.6 14.5 %multiply_add_fusion.6 = f32[8,8192]{1,0:T(8,128)S(1)} fusion(f32[8]{0:T(128)S(1)} %get-tuple-element.82, f32[8]{0:T(128)S(1)} %get-tuple-element.87, f32[8]{0:T(128)S(1)} %get-tuple-element.50, f32[8]{0:T(128)S(1)} %get-tuple-element.68, f32[8]{0:T(128)S(1)} %get-tuple-element.101, f32[8]{0:T(128)S(1)} %get-tuple-element.36, f32[8]{0:T(128)S(1)} %get-tuple-element.69, ...), kind=kLoop, calls=%fused_computation.132 | loop fusion | flops 5177344 | bytes 296448 | tf_op jit(solution)/shard_map/add | solution.py:106
  28.1 1.2 fusion.15
  29.3 1.2 fusion.17
  30.8 1.2 fusion.81
  32.0 1.2 fusion.82
  33.2 1.2 convolution_add_fusion.8
  34.5 1.2 convolution_subtract_fusion.4
  35.7 244.3 %all-gather.8.cloned.1.call-done = bf16[512,4096]{0,1:T(8,128)(2,1)} async-done(((bf16[512,64]{0,1:T(8,128)(2,1)}), bf16[512,4096]{0,1:T(8,128)(2,1)}) %all-gather.8.cloned.1.call-update) | async-done | bytes 4194320 | tf_op jit(solution)/shard_map/all_gather | solution.py:116
  280.0 15.9 %fusion.341 = f32[512,128]{1,0:T(8,128)S(1)} fusion(bf16[512,4096]{0,1:T(8,128)(2,1)} %all-gather.8.cloned.1.call-done, bf16[128,4096]{1,0:T(8,128)(2,1)} %param.10), kind=kOutput, calls=%fused_computation.435 | convolution fusion | flops 536870912 | bytes 5505024 | tf_op jit(solution)/shard_map/dot_general | solution.py:126
  296.0 289.6 %all-gather.4.cloned.1.call-done = bf16[4096,512]{1,0:T(8,128)(2,1)} async-done(((bf16[64,512]{1,0:T(8,128)(2,1)}), bf16[4096,512]{1,0:T(8,128)(2,1)}) %all-gather.4.cloned.1.call-update) | async-done | bytes 4194320 | tf_op jit(solution)/shard_map/all_gather | solution.py:83
  585.5 3.5 fusion.9
  589.7 6.2 all-to-all-start.2
  595.8 296.1 %all-gather.6.cloned.1.call-done = bf16[4096,512]{1,0:T(8,128)(2,1)} async-done(((bf16[64,512]{1,0:T(8,128)(2,1)}), bf16[4096,512]{1,0:T(8,128)(2,1)}) %all-gather.6.cloned.1.call-update) | async-done | bytes 4194320 | tf_op jit(solution)/shard_map/all_gather | solution.py:82
  891.9 4.1 fusion.10
  896.1 6.2 all-to-all-start
  902.4 1.2 fusion.11
  903.6 1.2 fusion.13
  904.8 6.8 all-to-all-done
  911.6 0.9 convert_bitcast_fusion.1
  912.5 1.2 fusion.19
  913.7 1.2 fusion.21
  914.9 1.2 fusion.80
  916.2 1.2 fusion.79
  917.4 1.2 fusion.84
  918.6 1.2 fusion.83
  919.8 1.2 convolution_subtract_fusion.2
  921.0 1.6 convolution_subtract_fusion.5
  922.6 1.2 convolution_add_fusion.9
  923.8 2.3 multiply_add_fusion
  929.6 0.9 fusion.30
  935.2 1.1 fusion.27
  936.3 0.9 fusion.6
  937.6 1.7 fusion.77
  939.3 14.0 %all_to_all.63 = bf16[8,64,128]{2,0,1:T(8,128)(2,1)} all-to-all(bf16[8,64,128]{2,0,1:T(8,128)(2,1)S(1)} %get-tuple-element.84), channel_id=1, replica_groups=mesh['ctx'=64,'tp'=8] {'ctx'}, dimensions={1} | all-to-all | bytes 262144 | tf_op jit(solution)/shard_map/all_to_all | solution.py:114
  953.3 5.5 all-to-all-start.3
  958.8 3.8 fusion.73
  962.7 5.4 all-to-all-done.3
  968.0 4.8 fusion.2
  972.9 4.8 fusion.1
  982.4 0.9 fusion.4
  983.7 4.0 multiply_reduce_fusion.3
  987.9 5.5 multiply_reduce_fusion.1
  993.4 5.5 multiply_reduce_fusion
  999.7 55.0 %reduce-scatter.5.cloned.1.call-done = bf16[512,128]{0,1:T(8,128)(2,1)} async-done(((bf16[4096,128]{0,1:T(8,128)(2,1)}), bf16[512,128]{0,1:T(8,128)(2,1)}) %reduce-scatter.5.cloned.1.call-update) | async-done | bytes 131088 | tf_op jit(solution)/shard_map/reduce_scatter | solution.py:145
  1054.7 43.9 %reduce-scatter.3.cloned.1.call-done = bf16[512,128]{0,1:T(8,128)(2,1)} async-done(((bf16[4096,128]{0,1:T(8,128)(2,1)}), bf16[512,128]{0,1:T(8,128)(2,1)}) %reduce-scatter.3.cloned.1.call-update) | async-done | bytes 131088 | tf_op jit(solution)/shard_map/reduce_scatter | solution.py:117
  (167 shorter events, 17.4 us)
Async XLA Ops:
  7.2 578.4 %copy-start = (bf16[128,4096]{1,0:T(8,128)(2,1)S(1)}, bf16[128,4096]{1,0:T(8,128)(2,1)}, u32[]{:S(2)}) copy-start(bf16[128,4096]{1,0:T(8,128)(2,1)} %param.9) | copy-start | bytes 3145732
  7.2 272.9 %all-gather.8.cloned.1.call-start = ((), (), s32[]{:S(2)}) async-start(), calls=%async_computation.8 | async-start | bytes 4259840 | tf_op jit(solution)/shard_map/all_gather | solution.py:116
  7.9 577.6 %all-gather.4.cloned.1.call-start = ((), (), s32[]{:S(2)}) async-start(), calls=%async_computation.6 | async-start | bytes 4259840 | tf_op jit(solution)/shard_map/all_gather | solution.py:83
  8.7 883.2 %all-gather.6.cloned.1.call-start = ((), (), s32[]{:S(2)}) async-start(), calls=%async_computation.7 | async-start | bytes 4259840 | tf_op jit(solution)/shard_map/all_gather | solution.py:82
  11.7 18.8 %copy-start.33 = (f32[8]{0:T(128)}, f32[8]{0:T(128)S(1)}, u32[]{:S(2)}) copy-start(f32[8]{0:T(128)S(1)} %get-tuple-element.67) | copy-start | bytes 100
  11.8 18.8 %copy-start.35 = (f32[8]{0:T(128)}, f32[8]{0:T(128)S(1)}, u32[]{:S(2)}) copy-start(f32[8]{0:T(128)S(1)} %get-tuple-element.69) | copy-start | bytes 100
  11.8 18.8 %copy-start.37 = (f32[8]{0:T(128)}, f32[8]{0:T(128)S(1)}, u32[]{:S(2)}) copy-start(f32[8]{0:T(128)S(1)} %get-tuple-element.73) | copy-start | bytes 100
  11.8 18.8 %copy-start.39 = (f32[8]{0:T(128)}, f32[8]{0:T(128)S(1)}, u32[]{:S(2)}) copy-start(f32[8]{0:T(128)S(1)} %get-tuple-element.80) | copy-start | bytes 100
  11.8 18.8 %copy-start.41 = (f32[8]{0:T(128)}, f32[8]{0:T(128)S(1)}, u32[]{:S(2)}) copy-start(f32[8]{0:T(128)S(1)} %get-tuple-element.81) | copy-start | bytes 100
  11.8 18.8 %copy-start.43 = (f32[8]{0:T(128)}, f32[8]{0:T(128)S(1)}, u32[]{:S(2)}) copy-start(f32[8]{0:T(128)S(1)} %get-tuple-element.82) | copy-start | bytes 100
  11.8 18.8 %copy-start.45 = (f32[8]{0:T(128)}, f32[8]{0:T(128)S(1)}, u32[]{:S(2)}) copy-start(f32[8]{0:T(128)S(1)} %get-tuple-element.68) | copy-start | bytes 100
  11.8 18.8 %copy-start.47 = (f32[8]{0:T(128)}, f32[8]{0:T(128)S(1)}, u32[]{:S(2)}) copy-start(f32[8]{0:T(128)S(1)} %get-tuple-element.71) | copy-start | bytes 100
  11.8 18.8 %copy-start.49 = (f32[8]{0:T(128)}, f32[8]{0:T(128)S(1)}, u32[]{:S(2)}) copy-start(f32[8]{0:T(128)S(1)} %get-tuple-element.72) | copy-start | bytes 100
  11.8 18.8 %copy-start.51 = (f32[8]{0:T(128)}, f32[8]{0:T(128)S(1)}, u32[]{:S(2)}) copy-start(f32[8]{0:T(128)S(1)} %get-tuple-element.77) | copy-start | bytes 100
  11.8 18.8 %copy-start.53 = (f32[8]{0:T(128)}, f32[8]{0:T(128)S(1)}, u32[]{:S(2)}) copy-start(f32[8]{0:T(128)S(1)} %get-tuple-element.78) | copy-start | bytes 100
  11.9 18.8 %copy-start.55 = (f32[8]{0:T(128)}, f32[8]{0:T(128)S(1)}, u32[]{:S(2)}) copy-start(f32[8]{0:T(128)S(1)} %get-tuple-element.79) | copy-start | bytes 100
  11.9 18.8 %copy-start.57 = (f32[8]{0:T(128)}, f32[8]{0:T(128)S(1)}, u32[]{:S(2)}) copy-start(f32[8]{0:T(128)S(1)} %get-tuple-element.70) | copy-start | bytes 100
  11.9 18.8 %copy-start.59 = (f32[8]{0:T(128)}, f32[8]{0:T(128)S(1)}, u32[]{:S(2)}) copy-start(f32[8]{0:T(128)S(1)} %get-tuple-element.74) | copy-start | bytes 100
  11.9 18.8 %copy-start.61 = (f32[8]{0:T(128)}, f32[8]{0:T(128)S(1)}, u32[]{:S(2)}) copy-start(f32[8]{0:T(128)S(1)} %get-tuple-element.75) | copy-start | bytes 100
  11.9 18.8 %copy-start.63 = (f32[8]{0:T(128)}, f32[8]{0:T(128)S(1)}, u32[]{:S(2)}) copy-start(f32[8]{0:T(128)S(1)} %get-tuple-element.76) | copy-start | bytes 100
  13.2 17.5 %copy-start.8 = (f32[8]{0:T(128)}, f32[8]{0:T(128)S(1)}, u32[]{:S(2)}) copy-start(f32[8]{0:T(128)S(1)} %get-tuple-element.100) | copy-start | bytes 100
  13.2 17.5 %copy-start.10 = (f32[8]{0:T(128)}, f32[8]{0:T(128)S(1)}, u32[]{:S(2)}) copy-start(f32[8]{0:T(128)S(1)} %get-tuple-element.102) | copy-start | bytes 100
  13.2 17.5 %copy-start.12 = (f32[8]{0:T(128)}, f32[8]{0:T(128)S(1)}, u32[]{:S(2)}) copy-start(f32[8]{0:T(128)S(1)} %get-tuple-element.90) | copy-start | bytes 100
  13.2 17.5 %copy-start.14 = (f32[8]{0:T(128)}, f32[8]{0:T(128)S(1)}, u32[]{:S(2)}) copy-start(f32[8]{0:T(128)S(1)} %get-tuple-element.91) | copy-start | bytes 100
  13.2 17.5 %copy-start.16 = (f32[8]{0:T(128)}, f32[8]{0:T(128)S(1)}, u32[]{:S(2)}) copy-start(f32[8]{0:T(128)S(1)} %get-tuple-element.92) | copy-start | bytes 100
  13.2 17.5 %copy-start.18 = (f32[8]{0:T(128)}, f32[8]{0:T(128)S(1)}, u32[]{:S(2)}) copy-start(f32[8]{0:T(128)S(1)} %get-tuple-element.97) | copy-start | bytes 100
  13.2 17.5 %copy-start.20 = (f32[8]{0:T(128)}, f32[8]{0:T(128)S(1)}, u32[]{:S(2)}) copy-start(f32[8]{0:T(128)S(1)} %get-tuple-element.98) | copy-start | bytes 100
  13.2 17.5 %copy-start.22 = (f32[8]{0:T(128)}, f32[8]{0:T(128)S(1)}, u32[]{:S(2)}) copy-start(f32[8]{0:T(128)S(1)} %get-tuple-element.101) | copy-start | bytes 100
  13.2 17.5 %copy-start.24 = (f32[8]{0:T(128)}, f32[8]{0:T(128)S(1)}, u32[]{:S(2)}) copy-start(f32[8]{0:T(128)S(1)} %get-tuple-element.93) | copy-start | bytes 100
  13.2 17.5 %copy-start.26 = (f32[8]{0:T(128)}, f32[8]{0:T(128)S(1)}, u32[]{:S(2)}) copy-start(f32[8]{0:T(128)S(1)} %get-tuple-element.94) | copy-start | bytes 100
  13.3 17.5 %copy-start.28 = (f32[8]{0:T(128)}, f32[8]{0:T(128)S(1)}, u32[]{:S(2)}) copy-start(f32[8]{0:T(128)S(1)} %get-tuple-element.95) | copy-start | bytes 100
  13.3 17.5 %copy-start.30 = (f32[8]{0:T(128)}, f32[8]{0:T(128)S(1)}, u32[]{:S(2)}) copy-start(f32[8]{0:T(128)S(1)} %get-tuple-element.99) | copy-start | bytes 100
  13.3 14.8 %copy-start.6 = (f32[8192]{0:T(1024)}, f32[8192]{0:T(1024)S(1)}, u32[]{:S(2)}) copy-start(f32[8192]{0:T(1024)S(1)} %iota_convert_fusion) | copy-start | bytes 98308
  295.9 600.1 %copy-start.3 = (f32[512,128]{1,0:T(8,128)}, f32[512,128]{1,0:T(8,128)S(1)}, u32[]{:S(2)}) copy-start(f32[512,128]{1,0:T(8,128)S(1)} %fusion.341) | copy-start | bytes 786436
  589.7 306.4 %all-to-all-start.2 = ((bf16[64,8,128]{2,1,0:T(8,128)(2,1)}), bf16[64,8,128]{2,1,0:T(8,128)(2,1)S(1)}, u32[]{:S(2)}, u32[]{:S(2)}) async-start(bf16[64,8,128]{2,1,0:T(8,128)(2,1)} %fusion.72), calls=%async_computation.3 | async-start | bytes 262144 | tf_op jit(solution)/shard_map/all_to_all | solution.py:131
  896.1 15.5 %all-to-all-start = ((bf16[64,8,128]{2,1,0:T(8,128)(2,1)}), bf16[64,8,128]{2,1,0:T(8,128)(2,1)}, u32[]{:S(2)}, u32[]{:S(2)}) async-start(bf16[64,8,128]{2,1,0:T(8,128)(2,1)} %fusion.10), calls=%async_computation | async-start | bytes 262144 | tf_op jit(solution)/shard_map/all_to_all | solution.py:92
  953.3 14.8 %all-to-all-start.3 = ((bf16[8,64,128]{2,0,1:T(8,128)(2,1)}), bf16[8,64,128]{2,0,1:T(8,128)(2,1)}, u32[]{:S(2)}, u32[]{:S(2)}) async-start(bf16[8,64,128]{2,0,1:T(8,128)(2,1)} %get-tuple-element.83), calls=%async_computation.4 | async-start | bytes 262144 | tf_op jit(solution)/shard_map/all_to_all | solution.py:144
  958.8 95.9 %reduce-scatter.5.cloned.1.call-start = ((), (), s32[]{:S(2)}) async-start(), calls=%async_computation.10 | async-start | bytes 1179648 | tf_op jit(solution)/shard_map/reduce_scatter | solution.py:145
  972.8 125.8 %reduce-scatter.3.cloned.1.call-start = ((), (), s32[]{:S(2)}) async-start(), calls=%async_computation.9 | async-start | bytes 1179648 | tf_op jit(solution)/shard_map/reduce_scatter | solution.py:117
  979.6 8.2 copy-start.13
  980.5 12.8 %copy-start.9 = (f32[8]{0:T(128)S(1)}, f32[8]{0:T(128)}, u32[]{:S(2)}) copy-start(f32[8]{0:T(128)} %copy-done.8) | copy-start | bytes 100
  980.6 12.8 %copy-start.11 = (f32[8]{0:T(128)S(1)}, f32[8]{0:T(128)}, u32[]{:S(2)}) copy-start(f32[8]{0:T(128)} %copy-done.10) | copy-start | bytes 100
  980.6 12.8 %copy-start.34 = (f32[8]{0:T(128)S(1)}, f32[8]{0:T(128)}, u32[]{:S(2)}) copy-start(f32[8]{0:T(128)} %copy-done.33) | copy-start | bytes 100
  980.6 12.8 %copy-start.36 = (f32[8]{0:T(128)S(1)}, f32[8]{0:T(128)}, u32[]{:S(2)}) copy-start(f32[8]{0:T(128)} %copy-done.35) | copy-start | bytes 100
  980.6 12.8 %copy-start.38 = (f32[8]{0:T(128)S(1)}, f32[8]{0:T(128)}, u32[]{:S(2)}) copy-start(f32[8]{0:T(128)} %copy-done.37) | copy-start | bytes 100
  980.6 12.8 %copy-start.40 = (f32[8]{0:T(128)S(1)}, f32[8]{0:T(128)}, u32[]{:S(2)}) copy-start(f32[8]{0:T(128)} %copy-done.39) | copy-start | bytes 100
  980.6 12.8 %copy-start.42 = (f32[8]{0:T(128)S(1)}, f32[8]{0:T(128)}, u32[]{:S(2)}) copy-start(f32[8]{0:T(128)} %copy-done.41) | copy-start | bytes 100
  980.6 12.8 %copy-start.44 = (f32[8]{0:T(128)S(1)}, f32[8]{0:T(128)}, u32[]{:S(2)}) copy-start(f32[8]{0:T(128)} %copy-done.43) | copy-start | bytes 100
  (25 other events, 152.6 us)
Sparse Core Ops, SparseCore 0:
  10.1 269.8 all-gather.7
  282.1 303.3 all-gather.3
  587.6 304.2 all-gather.5
  972.9 81.6 reduce-scatter.4
  1057.9 40.6 reduce-scatter.2
where the time goes:
time: 1120 us; the launch traced here: 1110 us
  waiting for transfers between devices  943 us (84%)
  matrix products  76 us (7%)
  other arithmetic  34.4 us (3%)
  starting transfers between devices  18.1 us (2%)
  between operations  15.5 us (1%)
  blocking collectives  14 us (1%)
    all_gather x1, waiting for transfers between devices, body(): value_full = lax.all_gather(w_value, 'ctx', axis=0, tiled=True)  296 us
    all_gather x1, waiting for transfers between devices, body(): query_full = lax.all_gather(w_query, 'ctx', axis=0, tiled=True)  290 us
    all_gather x1, waiting for transfers between devices, body(): out_full = lax.all_gather(w_out, 'ctx', axis=1, tiled=True)  244 us
    reduce_scatter x1, waiting for transfers between devices, body(): lax.psum_scatter((jnp.dot(query_full, grad_query, preferred_element_type=...  55 us
    reduce_scatter x1, waiting for transfers between devices, body(): lax.psum_scatter(lax.dot_general(out_full, gated, (((0,), (0,)), ((), ())...  43.9 us
  transfers between devices with their start and end apart: 8, of which 7 were waited for; matrix products, arithmetic and copies ran while one was open for 7% of the time, Pallas kernels for 0%

commit v1 on v0

v1 whole, which is shorter than its diff:
```python
import functools

import jax
import jax.numpy as jnp
from jax import lax
from jax.experimental import pallas as pl
from jax.experimental.pallas import tpu as pltpu
from jax.sharding import PartitionSpec as P

MESH = pl.DeviceIdType.MESH
F32, BF16 = jnp.float32, jnp.bfloat16
NX, NY, NZ = 4, 2, 8
NCTX, NTP = 64, 8
ROWS = 64
HALF = ROWS // 2
CG = 512
TOK = 128
CB = 8
ORDER = 16
LANES = CB * ORDER
NK = 13

NN = (((1,), (0,)), ((), ()))
NT = (((1,), (1,)), ((), ()))


def dot(a, b, dims=NN):
    return lax.dot_general(a, b, dims, preferred_element_type=F32)


def split(a):
    high = a.astype(BF16)
    return high, (a - high.astype(F32)).astype(BF16)


def build_tables(prm_ref, phi, plo, qhi, qlo, thi, tlo, bas):
    prm = prm_ref[...]
    row = lambda k: prm[k : k + 1, :]
    col = lambda k: jnp.broadcast_to(row(k), (LANES, LANES)).T
    d_row, f_row = row(0), row(1)
    d_col, f_col, r_col = col(0), col(1), col(2)
    lane = lax.broadcasted_iota(jnp.int32, (LANES, TOK), 1)
    sub = lax.broadcasted_iota(jnp.int32, (LANES, TOK), 0)
    t_q = (lane + 1).astype(F32)
    t_b = lane.astype(F32)
    t_p = (TOK - 1 - sub).astype(F32)
    mag = jnp.exp(-d_col * t_q)
    ang = f_col * t_q
    q_re, q_im = mag * jnp.cos(ang), mag * jnp.sin(ang)
    basis = jnp.exp(-d_col * t_b) * jnp.cos(f_col * t_b)
    bas[...] = basis
    mag = jnp.exp(-d_row * t_p)
    ang = f_row * t_p
    p_re, p_im = mag * jnp.cos(ang), mag * jnp.sin(ang)
    filt = jnp.sum((r_col * basis).reshape(CB, ORDER, TOK), axis=1)
    for c in range(CB):
        cols = slice(c * TOK, (c + 1) * TOK)
        own = lane // ORDER == c
        high, low = split(
            jnp.concatenate([jnp.where(own, p_re, 0.0), jnp.where(own, p_im, 0.0)], axis=1)
        )
        phi[cols, :] = high
        plo[cols, :] = low
        own = sub // ORDER == c
        high, low = split(
            jnp.concatenate([jnp.where(own, q_re, 0.0), jnp.where(own, q_im, 0.0)], axis=0)
        )
        qhi[:, cols] = high
        qlo[:, cols] = low
        rolled = pltpu.roll(
            jnp.broadcast_to(filt[c : c + 1, :], (TOK, TOK)), 0, 1, stride=1, stride_axis=0
        )
        skip = prm[3:4, c * ORDER : c * ORDER + 1]
        toep = jnp.where(lane >= sub, rolled, 0.0) + jnp.where(lane == sub, skip, 0.0)
        high, low = split(toep)
        thi[c] = high
        tlo[c] = low


def scan_chunks(re, im, lam, forward):
    at = lax.broadcasted_iota(jnp.int32, re.shape, 0)

    def shift(a, by):
        if forward:
            return jnp.where(at >= by, pltpu.roll(a, by, 0), 0.0)
        return jnp.where(at < NCTX - by, pltpu.roll(a, NCTX - by, 0), 0.0)

    re, im = shift(re, 1), shift(im, 1)
    by = 1
    for l_re, l_im in lam:
        s_re, s_im = shift(re, by), shift(im, by)
        re, im = re + l_re * s_re - l_im * s_im, im + l_re * s_im + l_im * s_re
        by *= 2
    return re, im


def convolve(prm_ref, x32, y32, phi, plo, qhi, qlo, thi, tlo, bas, res_ref):
    prm = prm_ref[...]
    d_row, f_row, r_row = prm[0:1, :], prm[1:2, :], prm[2:3, :]
    lam = []
    for k in range(6):
        span = float(TOK * 2**k)
        mag = jnp.exp(-d_row * span)
        lam.append((mag * jnp.cos(f_row * span), mag * jnp.sin(f_row * span)))
    xs = [x32[pl.ds(c, NCTX, stride=2 * CB), :].astype(BF16) for c in range(CB)]
    gs = [x32[pl.ds(CB + c, NCTX, stride=2 * CB), :].astype(BF16) for c in range(CB)]
    xcat = jnp.concatenate(xs, axis=1)
    gcat = jnp.concatenate(gs, axis=1)
    e = dot(xcat, phi[...]) + dot(xcat, plo[...])
    f = dot(gcat, qhi[...], NT) + dot(gcat, qlo[...], NT)
    h_re, h_im = scan_chunks(e[:, :LANES], e[:, LANES:], lam, True)
    k_re, k_im = scan_chunks(f[:, :LANES], f[:, LANES:], lam, False)
    across = jnp.sum(h_re * f[:, :LANES] - h_im * f[:, LANES:], axis=0, keepdims=True)
    hh, hl = split(jnp.concatenate([r_row * h_re, -r_row * h_im], axis=1))
    kh, kl = split(jnp.concatenate([r_row * k_re, -r_row * k_im], axis=1))
    y = dot(hh, qhi[...]) + dot(hl, qhi[...]) + dot(hh, qlo[...])
    z = dot(kh, phi[...], NT) + dot(kl, phi[...], NT) + dot(kh, plo[...], NT)
    lane = lax.broadcasted_iota(jnp.int32, (TOK, TOK), 1)
    sub = lax.broadcasted_iota(jnp.int32, (TOK, TOK), 0)
    flip = jnp.where(lane + sub == TOK - 1, 1.0, 0.0).astype(BF16)
    corr = []
    for c in range(CB):
        cols = slice(c * TOK, (c + 1) * TOK)
        yc = y[:, cols] + dot(xs[c], thi[c]) + dot(xs[c], tlo[c])
        zc = z[:, cols] + dot(gs[c], thi[c], NT) + dot(gs[c], tlo[c], NT)
        y32[pl.ds(c, NCTX, stride=2 * CB), :] = yc
        y32[pl.ds(CB + c, NCTX, stride=2 * CB), :] = zc
        back_t = dot(xs[c], flip).T.astype(BF16)
        pairs = dot(back_t, gs[c])
        lagged = pltpu.roll(pairs, 1, 1, stride=1, stride_axis=0)
        corr.append(jnp.sum(jnp.where(lane <= sub, lagged, 0.0), axis=0, keepdims=True))
    spread = jnp.concatenate([jnp.broadcast_to(a, (ORDER, TOK)) for a in corr], axis=0)
    within = jnp.sum((spread * bas[...]).T, axis=0, keepdims=True)
    res_ref[...] = jnp.broadcast_to(within + across, res_ref.shape)


def kernel(
    f_ref,
    g_ref,
    wv_ref,
    wq_ref,
    wo_ref,
    prm_ref,
    mixed_ref,
    gin_ref,
    res_ref,
    w,
    acc,
    query,
    gg,
    snd,
    rcv,
    snd2,
    rcv2,
    x32,
    y32,
    phi,
    plo,
    qhi,
    qlo,
    thi,
    tlo,
    bas,
    part,
    got,
    ssem,
    rsem,
    xsem,
    psem,
):
    ctx = lax.axis_index("ctx")
    tp = lax.axis_index("tp")
    xy = ctx // NZ
    x, y, z = xy // NY, xy % NY, ctx % NZ
    xl, xr = (x + NX - 1) % NX, (x + 1) % NX
    zl, zr = (z + NZ - 1) % NZ, (z + 1) % NZ
    yo = 1 - y

    barrier = pltpu.get_barrier_semaphore()

    def greet_ctx(k, carry):
        pl.semaphore_signal(
            barrier, inc=1, device_id=((ctx + k) % NCTX, tp), device_id_type=MESH
        )
        return carry

    def greet_tp(k, carry):
        pl.semaphore_signal(barrier, inc=1, device_id=(ctx, (tp + k) % NTP), device_id_type=MESH)
        return carry

    lax.fori_loop(1, NCTX, greet_ctx, 0)
    lax.fori_loop(1, NTP, greet_tp, 0)
    for i, ref in enumerate((wv_ref, wq_ref, wo_ref)):
        w[i, xy, z] = ref[...]
    pl.semaphore_wait(barrier, NCTX + NTP - 2)

    def dev(xi, yi, zi):
        return ((xi * NY + yi) * NZ + zi, tp)

    def copy(half, i, k, ref, device):
        return pltpu.make_async_remote_copy(
            src_ref=ref,
            dst_ref=ref,
            send_sem=ssem.at[half, i, k],
            recv_sem=rsem.at[half, i, k],
            device_id=device,
            device_id_type=MESH,
        )

    to_y, to_r, to_l = dev(x, yo, z), dev(xr, y, z), dev(xl, y, z)
    to_u, to_d = dev(x, y, zr), dev(x, y, zl)

    first, second = pl.ds(0, HALF), pl.ds(HALF, HALF)
    a_own = lambda i, yi: w.at[i, x * NY + yi, z, first]
    a_pair = lambda i, xi: w.at[i, pl.ds(xi * NY, NY), z, first]
    a_one = lambda i, xi, yi: w.at[i, xi * NY + yi, z, first]

    def a_plane(i, step, up, whole):
        zi = (z + NZ - step) % NZ if up else (z + step) % NZ
        if whole:
            return w.at[i, :, zi, first]
        return w.at[i, pl.ds(0 if up else NX, NX), zi, first]

    def b_block(i, step, up, whole):
        zi = (z + NZ - step) % NZ if up else (z + step) % NZ
        rows = second if whole else pl.ds(HALF if up else HALF + HALF // 2, HALF // 2)
        return w.at[i, xy, zi, rows]

    b_line = lambda i, yi: w.at[i, x * NY + yi, :, second]
    b_pair = lambda i, xi: w.at[i, pl.ds(xi * NY, NY), :, second]
    b_one = lambda i, xi, yi: w.at[i, xi * NY + yi, :, second]
    x2 = (x + 2) % NX

    def a_copy(i, k):
        if k == 0:
            return a_own(i, y), to_y, a_own(i, yo)
        if k == 1:
            return a_pair(i, x), to_r, a_pair(i, xl)
        if k == 2:
            return a_pair(i, x), to_l, a_pair(i, xr)
        if k == 3:
            return a_one(i, xl, 0), to_r, a_one(i, x2, 0)
        if k == 4:
            return a_one(i, xr, 1), to_l, a_one(i, x2, 1)
        up, step = k < 9, (k - 5) % 4
        whole = step < 3
        return a_plane(i, step, up, whole), to_u if up else to_d, a_plane(i, step + 1, up, whole)

    def b_copy(i, k):
        if k == 8:
            return b_line(i, y), to_y, b_line(i, yo)
        if k == 9:
            return b_pair(i, x), to_r, b_pair(i, xl)
        if k == 10:
            return b_pair(i, x), to_l, b_pair(i, xr)
        if k == 11:
            return b_one(i, xl, 0), to_r, b_one(i, x2, 0)
        if k == 12:
            return b_one(i, xr, 1), to_l, b_one(i, x2, 1)
        up, step = k < 4, k % 4
        whole = step < 3
        return b_block(i, step, up, whole), to_u if up else to_d, b_block(i, step + 1, up, whole)

    makers = (a_copy, b_copy)

    def start(half, i, *ks):
        for k in ks:
            out, device, _ = makers[half](i, k)
            copy(half, i, k, out, device).start()

    def arrive(half, i, *ks):
        for k in ks:
            _, device, incoming = makers[half](i, k)
            copy(half, i, k, incoming, device).wait_recv()

    every = range(3)
    for i in every:
        start(0, i, 0)
        start(1, i, 0, 4)
    for i in every:
        arrive(0, i, 0)
        start(0, i, 1, 2)
        arrive(1, i, 0, 4)
        start(1, i, 1, 5)
    for i in every:
        arrive(0, i, 1)
        start(0, i, 3)
        arrive(0, i, 2)
        start(0, i, 4)
        arrive(1, i, 1, 5)
        start(1, i, 2, 6)
    for i in every:
        arrive(0, i, 3, 4)
        start(0, i, 5, 9)
        arrive(1, i, 2, 6)
        start(1, i, 3, 7)
    build_tables(prm_ref, phi, plo, qhi, qlo, thi, tlo, bas)
    for i in every:
        arrive(1, i, 3, 7)
        start(1, i, 8)

    def a_next(i, step):
        arrive(0, i, 5 + step, 9 + step)
        start(0, i, 6 + step, 10 + step)

    def b_first(i):
        arrive(1, i, 8)
        start(1, i, 9, 10)

    def b_second(i):
        arrive(1, i, 9)
        start(1, i, 11)
        arrive(1, i, 10)
        start(1, i, 12)

    a_next(0, 0)
    b_first(0)
    a_next(1, 0)
    b_first(1)
    a_next(2, 0)
    b_first(2)
    b_second(0)
    a_next(0, 1)
    a_next(1, 1)
    b_second(1)
    a_next(2, 1)
    a_next(0, 2)
    b_second(2)
    a_next(1, 2)
    a_next(2, 2)

    def project(lhs_ref, i):
        acc[...] = jnp.zeros_like(acc)

        def step(kb, carry):
            cols = pl.ds(pl.multiple_of(kb * CG, CG), CG)
            acc[...] += dot(lhs_ref[:, cols], w[i, kb].reshape(CG, CG))
            return carry

        lax.fori_loop(0, NCTX // NZ, step, 0)

    def finish(i):
        arrive(0, i, 8, 12)
        arrive(1, i, 11, 12)

    finish(0)
    project(f_ref, 0)
    value_t = acc[...].T.reshape(NCTX, CB, TOK)
    x32[...] = jnp.concatenate([value_t, value_t], axis=1).reshape(x32.shape)
    finish(1)
    project(f_ref, 1)
    query[...] = acc[...].astype(BF16).astype(F32)
    finish(2)
    project(g_ref, 2)
    gg[...] = acc[...]
    grad_t = (acc[...] * query[...]).T.reshape(NCTX, CB, TOK)
    both = jnp.concatenate([x32[...].reshape(NCTX, 2 * CB, TOK)[:, :CB], grad_t], axis=1)
    snd[...] = both.astype(BF16)

    def exchange(src, dst, which):
        def one(k, carry):
            to = (ctx + k) % NCTX
            pltpu.make_async_remote_copy(
                src_ref=src.at[to],
                dst_ref=dst.at[ctx],
                send_sem=xsem.at[which, 0],
                recv_sem=xsem.at[which, 1],
                device_id=(to, tp),
                device_id_type=MESH,
            ).start()
            return carry

        lax.fori_loop(1, NCTX, one, 0)
        dst[ctx] = src[ctx]
        rest = dst.at[pl.ds(0, NCTX - 1)]
        pltpu.make_async_copy(rest, rest, xsem.at[which, 1]).wait()

    def sent(src, which):
        rest = src.at[pl.ds(0, NCTX - 1)]
        pltpu.make_async_copy(rest, rest, xsem.at[which, 0]).wait()

    exchange(snd, rcv, 0)
    x32[...] = rcv[...].astype(F32).reshape(x32.shape)
    convolve(prm_ref, x32, y32, phi, plo, qhi, qlo, thi, tlo, bas, res_ref)
    snd2[...] = y32[...].reshape(snd2.shape).astype(BF16)
    exchange(snd2, rcv2, 1)

    back = rcv2[...].astype(F32)
    state = back[:, :CB].reshape(CG, TOK).T
    grad_value = back[:, CB:].reshape(CG, TOK).T.astype(BF16)
    gated = (query[...] * state).astype(BF16)
    grad_query = (gg[...] * state).astype(BF16)

    def scatter(which, block):
        def one(k, carry):
            to = (tp + k) % NTP
            part[which, to] = block(to).astype(BF16)

            @pl.when(k < NTP)
            def _():
                pltpu.make_async_remote_copy(
                    src_ref=part.at[which, to],
                    dst_ref=got.at[which, tp],
                    send_sem=psem.at[which, 0],
                    recv_sem=psem.at[which, 1],
                    device_id=(ctx, to),
                    device_id_type=MESH,
                ).start()

            return carry

        lax.fori_loop(1, NTP + 1, one, 0)
        got[which, tp] = part[which, tp]

    def collect(which, out):
        rest = got.at[which, pl.ds(0, NTP - 1)]
        pltpu.make_async_copy(rest, rest, psem.at[which, 1]).wait()
        total = got[which, 0].astype(F32)
        for k in range(1, NTP):
            total += got[which, k].astype(F32)
        out[...] = total.astype(BF16)

    scatter(0, lambda q: dot(gated, w[2, q].reshape(CG, CG), NT))
    scatter(
        1,
        lambda q: dot(grad_query, w[1, q].reshape(CG, CG), NT)
        + dot(grad_value, w[0, q].reshape(CG, CG), NT),
    )
    collect(0, mixed_ref)
    collect(1, gin_ref)

    sent(snd, 0)
    sent(snd2, 1)
    for which in range(2):
        rest = part.at[which, pl.ds(0, NTP - 1)]
        pltpu.make_async_copy(rest, rest, psem.at[which, 0]).wait()
    for half in range(2):
        for i in every:
            for k in range(NK):
                out, device, _ = makers[half](i, k)
                copy(half, i, k, out, device).wait_send()


def body(features, grad_out, w_value, w_query, w_out, residues, decays, freqs, skips):
    first = lax.axis_index("ctx") * CB
    own = lambda a: lax.dynamic_slice_in_dim(a, first, CB, a.ndim - 1)
    flat = lambda a: own(a).T.reshape(1, LANES)
    skip_row = jnp.broadcast_to(own(skips)[:, None], (CB, ORDER)).reshape(1, LANES)
    prm = jnp.concatenate(
        [flat(decays), flat(freqs), flat(residues), skip_row, jnp.zeros((4, LANES), F32)], axis=0
    )
    vmem = pl.BlockSpec(memory_space=pltpu.VMEM)
    scratch = [
        pltpu.VMEM((3, NX * NY, NZ, ROWS, CG), BF16),
        pltpu.VMEM((TOK, CG), F32),
        pltpu.VMEM((TOK, CG), F32),
        pltpu.VMEM((TOK, CG), F32),
        pltpu.VMEM((NCTX, 2 * CB, TOK), BF16),
        pltpu.VMEM((NCTX, 2 * CB, TOK), BF16),
        pltpu.VMEM((NCTX, 2 * CB, TOK), BF16),
        pltpu.VMEM((NCTX, 2 * CB, TOK), BF16),
        pltpu.VMEM((NCTX * 2 * CB, TOK), F32),
        pltpu.VMEM((NCTX * 2 * CB, TOK), F32),
        pltpu.VMEM((CB * TOK, 2 * LANES), BF16),
        pltpu.VMEM((CB * TOK, 2 * LANES), BF16),
        pltpu.VMEM((2 * LANES, CB * TOK), BF16),
        pltpu.VMEM((2 * LANES, CB * TOK), BF16),
        pltpu.VMEM((CB, TOK, TOK), BF16),
        pltpu.VMEM((CB, TOK, TOK), BF16),
        pltpu.VMEM((LANES, TOK), F32),
        pltpu.VMEM((2, NTP, TOK, CG), BF16),
        pltpu.VMEM((2, NTP, TOK, CG), BF16),
        pltpu.SemaphoreType.DMA((2, 3, NK)),
        pltpu.SemaphoreType.DMA((2, 3, NK)),
        pltpu.SemaphoreType.DMA((2, 2)),
        pltpu.SemaphoreType.DMA((2, 2)),
    ]
    mixed, grad_in, res = pl.pallas_call(
        kernel,
        out_shape=(
            jax.ShapeDtypeStruct((TOK, CG), BF16),
            jax.ShapeDtypeStruct((TOK, CG), BF16),
            jax.ShapeDtypeStruct((8, LANES), F32),
        ),
        in_specs=[vmem] * 6,
        out_specs=(vmem,) * 3,
        scratch_shapes=scratch,
        compiler_params=pltpu.CompilerParams(
            collective_id=0, has_side_effects=True, vmem_limit_bytes=48 * 2**20
        ),
        cost_estimate=pl.CostEstimate(
            flops=2 * 6 * TOK * CG * 4096, bytes_accessed=2**22, transcendentals=2**17
        ),
    )(features, grad_out, w_value, w_query, w_out.T, prm)
    return mixed, grad_in, res[0].reshape(CB, ORDER).T


def solution(mesh):
    placed = (
        P("ctx", None),
        P("ctx", None),
        P("ctx", "tp"),
        P("ctx", "tp"),
        P("tp", "ctx"),
        P(None, "tp"),
        P(None, "tp"),
        P(None, "tp"),
        P("tp"),
    )
    return jax.shard_map(
        body,
        mesh=mesh,
        in_specs=placed,
        out_specs=(P("ctx", "tp"), P("ctx", "tp"), P(None, ("tp", "ctx"))),
        check_vma=False,
    )
```

time: 1120 us -> 173 us (0.15); the launches traced: 1110 us -> 173 us
  waiting for transfers between devices: 943 us -> 0 us
  Pallas kernels: 0 us -> 164 us
  matrix products: 76 us -> 0 us
  other arithmetic: 34.4 us -> 0 us
  starting transfers between devices: 18.1 us -> 0 us
  between operations: 15.5 us -> 0.71 us
  blocking collectives: 14 us -> 0 us
    all_gather x3 -> x0, waiting for transfers between devices: 830 us -> none  [the longest x1 296 us: body(): value_full = lax.all_gather(w_value, 'ctx', axis=0, tiled=True)]
    pallas_call x0 -> x1, Pallas kernels: none -> 164 us  [body(): pl.pallas_call(kernel, out_shape=(jax.ShapeDtypeStruct((TOK, CG), BF16),...]
    reduce_scatter x2 -> x0, waiting for transfers between devices: 99 us -> none  [the longest x1 55 us: body(): lax.psum_scatter((jnp.dot(query_full, grad_query, preferred_element_type=...]
    dot_general x42 -> x0, matrix products: 76 us -> none  [the longest x1 15.9 us: body(): lax.dot_general(out_full, grad_out, (((1,), (1,)), ((), ())), preferred_e...]
    all_to_all x3 -> x0, starting transfers between devices: 17.9 us -> none  [the longest x1 6.23 us: body(): lax.all_to_all(value_t, 'ctx', split_axis=0, concat_axis=1, tiled=True)]
    reduce_sum x3 -> x0, other arithmetic: 15 us -> none  [body(): jnp.sum(grad_filt * basis, axis=1)]
    add x1 -> x0, other arithmetic: 14.5 us -> none  [body(): filt = filt + res_blk[mode][:, None] * basis]
    all_to_all x1 -> x0, blocking collectives: 14 us -> none  [body(): lax.all_to_all(state_chan, 'ctx', split_axis=1, concat_axis=0, tiled=True)]
  transfers between devices with their start and end apart: 8 -> 0, of which waited for: 7 -> 0; matrix products, arithmetic and copies ran while one was open for 7% -> 0% of each run, Pallas kernels for 0% -> 0%
where the time goes in v1:
time: 173 us
  Pallas kernels  164 us (95%)
  local copies, waits for them, and re-layouts  7.6 us (4%)
    pallas_call x1, Pallas kernels, body(): pl.pallas_call(kernel, out_shape=(jax.ShapeDtypeStruct((TOK, CG), BF16),...  164 us
    unnamed x14, local copies, waits for them, and re-layouts  4.61 us

profile of v1, /device:TPU:1, one launch (start us, length us, event | category | flops | bytes accessed | tf_op | source)
XLA Modules:
  0.0 172.6 jit_solution(2501298798209249693)
XLA Ops:
  0.6 0.0 copy-start
  0.7 0.0 copy-start.4
  0.7 0.0 copy-start.3
  0.7 0.8 dynamic_slice.15
  1.5 0.1 broadcast_in_dim.4
  1.5 0.1 reshape.22
  1.6 0.0 copy-done
  1.6 0.1 dynamic-slice_bitcast_fusion.2
  1.7 0.1 copy.12
  1.8 0.1 reshape.19
  1.8 0.8 dynamic-slice_bitcast_fusion
  2.6 0.1 copy.14
  2.7 0.1 reshape.21
  2.8 0.1 copy.13
  2.9 0.1 reshape.20
  3.0 0.0 copy-done.4
  3.0 0.0 copy-done.3
  3.0 0.0 copy-start.1
  3.0 1.2 copy-done.1
  4.2 0.0 copy-start.2
  4.2 1.2 copy-done.2
  5.4 0.0 copy-start.5
  5.5 0.8 copy-done.5
  6.3 164.3 %shard_map.112 = (bf16[128,512]{1,0:T(8,128)(2,1)S(1)}, bf16[128,512]{1,0:T(8,128)(2,1)S(1)}, f32[8,128]{1,0:T(8,128)S(1)}) custom-call(bf16[128,4096]{1,0:T(8,128)(2,1)S(1)} %copy-done.1, bf16[128,4096]{1,0:T(8,128)(2,1)S(1)} %copy-done.2, bf16[64,512]{1,0:T(8,128)(2,1)S(1)} %copy-done.3, bf16[64,512]{1,0:T(8,128)(2,1)S(1)} %copy-done.4, ...), custom_call_target="tpu_custom_call" | custom-call | flops 3221225472 | bytes 4194304 | tf_op jit(solution)/shard_map/pallas_call | solution.py:478
  170.6 0.7 reshape_squeeze.3
  171.3 0.7 copy.17
  171.9 0.7 copy.18
  (3 shorter events, 0.0 us)
Async XLA Ops:
  0.6 1.0 copy-start
  0.7 2.3 %copy-start.4 = (bf16[64,512]{1,0:T(8,128)(2,1)S(1)}, bf16[64,512]{1,0:T(8,128)(2,1)}, u32[]{:S(2)}) copy-start(bf16[64,512]{1,0:T(8,128)(2,1)} %wq_ref.1) | copy-start | bytes 196612
  0.7 2.3 %copy-start.3 = (bf16[64,512]{1,0:T(8,128)(2,1)S(1)}, bf16[64,512]{1,0:T(8,128)(2,1)}, u32[]{:S(2)}) copy-start(bf16[64,512]{1,0:T(8,128)(2,1)} %wv_ref.1) | copy-start | bytes 196612
  3.0 1.2 copy-start.1
  4.2 1.2 copy-start.2
  5.4 0.8 copy-start.5

commit v2 on v1

--- a/solution.py
+++ b/solution.py
@@ -18,7 +18,7 @@
 CB = 8
 ORDER = 16
 LANES = CB * ORDER
-NK = 13
+NK = 12
 
 NN = (((1,), (0,)), ((), ()))
 NT = (((1,), (1,)), ((), ()))
@@ -145,7 +145,11 @@
     gin_ref,
     res_ref,
     w,
+    lhs,
     acc,
+    own,
+    psnd,
+    prcv,
     query,
     gg,
     snd,
@@ -161,41 +165,80 @@
     thi,
     tlo,
     bas,
+    pair,
     part,
+    sib,
+    summed,
     got,
     ssem,
     rsem,
+    lsem,
+    fsem,
+    ysem,
     xsem,
+    csem,
     psem,
 ):
     ctx = lax.axis_index("ctx")
     tp = lax.axis_index("tp")
     xy = ctx // NZ
     x, y, z = xy // NY, xy % NY, ctx % NZ
-    xl, xr = (x + NX - 1) % NX, (x + 1) % NX
+    y_hi, core = tp // 2, tp % 2
+    xl, xr, x2 = (x + NX - 1) % NX, (x + 1) % NX, (x + 2) % NX
     zl, zr = (z + NZ - 1) % NZ, (z + 1) % NZ
     yo = 1 - y
+    at = lambda xi, yi, zi: (xi * NY + yi) * NZ + zi
+    partner = (at(x, yo, z), tp)
+    sibling = (ctx, y_hi * 2 + 1 - core)
+    sum_ctx = at(x, core, z)
+    to_self = core == y
 
     barrier = pltpu.get_barrier_semaphore()
 
+    def greet(device):
+        pl.semaphore_signal(barrier, inc=1, device_id=device, device_id_type=MESH)
+
     def greet_ctx(k, carry):
-        pl.semaphore_signal(
-            barrier, inc=1, device_id=((ctx + k) % NCTX, tp), device_id_type=MESH
-        )
+        greet(((ctx + k) % NCTX, tp))
         return carry
 
-    def greet_tp(k, carry):
-        pl.semaphore_signal(barrier, inc=1, device_id=(ctx, (tp + k) % NTP), device_id_type=MESH)
-        return carry
-
     lax.fori_loop(1, NCTX, greet_ctx, 0)
-    lax.fori_loop(1, NTP, greet_tp, 0)
+    greet(sibling)
+    for k in range(1, NX):
+        greet((sum_ctx, (y_hi + k) % NX * 2 + y))
+
+    @pl.when(jnp.logical_not(to_self))
+    def _():
+        greet((sum_ctx, y_hi * 2 + y))
+
+    def columns(block):
+        return pl.ds(pl.multiple_of(block * CG, CG), CG)
+
+    def token_rows(yi):
+        return pl.ds(pl.multiple_of(yi * TOK, TOK), TOK)
+
     for i, ref in enumerate((wv_ref, wq_ref, wo_ref)):
-        w[i, xy, z] = ref[...]
-    pl.semaphore_wait(barrier, NCTX + NTP - 2)
-
-    def dev(xi, yi, zi):
-        return ((xi * NY + yi) * NZ + zi, tp)
+        w[i, x, z] = ref[...]
+    for a, ref in enumerate((f_ref, g_ref)):
+        for b in range(NX):
+            pltpu.make_async_copy(
+                ref.at[:, columns(b * NY + y)], lhs.at[a, b, token_rows(y)], lsem.at[a, b]
+            ).start()
+    pl.semaphore_wait(barrier, NCTX - 1 + 1 + NX - 1 + jnp.where(to_self, 0, 1))
+
+    def swap(a, b):
+        return pltpu.make_async_remote_copy(
+            src_ref=(f_ref, g_ref)[a].at[:, columns(b * NY + yo)],
+            dst_ref=lhs.at[a, b, token_rows(y)],
+            send_sem=fsem.at[0, a, b],
+            recv_sem=fsem.at[1, a, b],
+            device_id=partner,
+            device_id_type=MESH,
+        )
+
+    for a in range(2):
+        for b in range(NX):
+            swap(a, b).start()
 
     def copy(half, i, k, ref, device):
         return pltpu.make_async_remote_copy(
@@ -207,59 +250,45 @@
             device_id_type=MESH,
         )
 
-    to_y, to_r, to_l = dev(x, yo, z), dev(xr, y, z), dev(xl, y, z)
-    to_u, to_d = dev(x, y, zr), dev(x, y, zl)
-
+    to_r, to_l = (at(xr, y, z), tp), (at(xl, y, z), tp)
+    to_u, to_d = (at(x, y, zr), tp), (at(x, y, zl), tp)
+    quarter = HALF // 2
     first, second = pl.ds(0, HALF), pl.ds(HALF, HALF)
-    a_own = lambda i, yi: w.at[i, x * NY + yi, z, first]
-    a_pair = lambda i, xi: w.at[i, pl.ds(xi * NY, NY), z, first]
-    a_one = lambda i, xi, yi: w.at[i, xi * NY + yi, z, first]
-
-    def a_plane(i, step, up, whole):
-        zi = (z + NZ - step) % NZ if up else (z + step) % NZ
-        if whole:
-            return w.at[i, :, zi, first]
-        return w.at[i, pl.ds(0 if up else NX, NX), zi, first]
-
-    def b_block(i, step, up, whole):
-        zi = (z + NZ - step) % NZ if up else (z + step) % NZ
-        rows = second if whole else pl.ds(HALF if up else HALF + HALF // 2, HALF // 2)
-        return w.at[i, xy, zi, rows]
-
-    b_line = lambda i, yi: w.at[i, x * NY + yi, :, second]
-    b_pair = lambda i, xi: w.at[i, pl.ds(xi * NY, NY), :, second]
-    b_one = lambda i, xi, yi: w.at[i, xi * NY + yi, :, second]
-    x2 = (x + 2) % NX
+
+    def z_from(step, up):
+        return (z + NZ - step) % NZ if up else (z + step) % NZ
 
     def a_copy(i, k):
-        if k == 0:
-            return a_own(i, y), to_y, a_own(i, yo)
-        if k == 1:
-            return a_pair(i, x), to_r, a_pair(i, xl)
-        if k == 2:
-            return a_pair(i, x), to_l, a_pair(i, xr)
-        if k == 3:
-            return a_one(i, xl, 0), to_r, a_one(i, x2, 0)
-        if k == 4:
-            return a_one(i, xr, 1), to_l, a_one(i, x2, 1)
-        up, step = k < 9, (k - 5) % 4
-        whole = step < 3
-        return a_plane(i, step, up, whole), to_u if up else to_d, a_plane(i, step + 1, up, whole)
+        if k < 2:
+            return w.at[i, x, z, first], (to_r, to_l)[k], w.at[i, (xl, xr)[k], z, first]
+        if k < 4:
+            rows = pl.ds((k - 2) * quarter, quarter)
+            return w.at[i, (xl, xr)[k - 2], z, rows], (to_r, to_l)[k - 2], w.at[i, x2, z, rows]
+        up, step = k < 8, k % 4
+        some = slice(None) if step < 3 else pl.ds(0 if up else NX // 2, NX // 2)
+        return (
+            w.at[i, some, z_from(step, up), first],
+            to_u if up else to_d,
+            w.at[i, some, z_from(step + 1, up), first],
+        )
 
     def b_copy(i, k):
-        if k == 8:
-            return b_line(i, y), to_y, b_line(i, yo)
-        if k == 9:
-            return b_pair(i, x), to_r, b_pair(i, xl)
-        if k == 10:
-            return b_pair(i, x), to_l, b_pair(i, xr)
-        if k == 11:
-            return b_one(i, xl, 0), to_r, b_one(i, x2, 0)
-        if k == 12:
-            return b_one(i, xr, 1), to_l, b_one(i, x2, 1)
-        up, step = k < 4, k % 4
-        whole = step < 3
-        return b_block(i, step, up, whole), to_u if up else to_d, b_block(i, step + 1, up, whole)
+        if k < 8:
+            up, step = k < 4, k % 4
+            rows = second if step < 3 else pl.ds(HALF if up else HALF + quarter, quarter)
+            return (
+                w.at[i, x, z_from(step, up), rows],
+                to_u if up else to_d,
+                w.at[i, x, z_from(step + 1, up), rows],
+            )
+        if k < 10:
+            return w.at[i, x, :, second], (to_r, to_l)[k - 8], w.at[i, (xl, xr)[k - 8], :, second]
+        some = pl.ds((k - 10) * (NZ // 2), NZ // 2)
+        return (
+            w.at[i, (xl, xr)[k - 10], some, second],
+            (to_r, to_l)[k - 10],
+            w.at[i, x2, some, second],
+        )
 
     makers = (a_copy, b_copy)
 
@@ -275,50 +304,40 @@
 
     every = range(3)
     for i in every:
-        start(0, i, 0)
+        start(0, i, 0, 1)
         start(1, i, 0, 4)
     for i in every:
         arrive(0, i, 0)
-        start(0, i, 1, 2)
+        start(0, i, 2)
+        arrive(0, i, 1)
+        start(0, i, 3)
         arrive(1, i, 0, 4)
         start(1, i, 1, 5)
     for i in every:
-        arrive(0, i, 1)
-        start(0, i, 3)
-        arrive(0, i, 2)
-        start(0, i, 4)
+        arrive(0, i, 2, 3)
+        start(0, i, 4, 8)
         arrive(1, i, 1, 5)
         start(1, i, 2, 6)
     for i in every:
-        arrive(0, i, 3, 4)
-        start(0, i, 5, 9)
         arrive(1, i, 2, 6)
         start(1, i, 3, 7)
-    build_tables(prm_ref, phi, plo, qhi, qlo, thi, tlo, bas)
     for i in every:
         arrive(1, i, 3, 7)
-        start(1, i, 8)
+        start(1, i, 8, 9)
 
     def a_next(i, step):
-        arrive(0, i, 5 + step, 9 + step)
-        start(0, i, 6 + step, 10 + step)
-
-    def b_first(i):
+        arrive(0, i, 4 + step, 8 + step)
+        start(0, i, 5 + step, 9 + step)
+
+    def b_second(i):
         arrive(1, i, 8)
-        start(1, i, 9, 10)
-
-    def b_second(i):
+        start(1, i, 10)
         arrive(1, i, 9)
         start(1, i, 11)
-        arrive(1, i, 10)
-        start(1, i, 12)
-
-    a_next(0, 0)
-    b_first(0)
-    a_next(1, 0)
-    b_first(1)
-    a_next(2, 0)
-    b_first(2)
+
+    for i in every:
+        a_next(i, 0)
+    build_tables(prm_ref, phi, plo, qhi, qlo, thi, tlo, bas)
     b_second(0)
     a_next(0, 1)
     a_next(1, 1)
@@ -329,31 +348,58 @@
     a_next(1, 2)
     a_next(2, 2)
 
-    def project(lhs_ref, i):
+    def give(i):
+        return pltpu.make_async_remote_copy(
+            src_ref=psnd.at[i],
+            dst_ref=prcv.at[i],
+            send_sem=ysem.at[0, i],
+            recv_sem=ysem.at[1, i],
+            device_id=partner,
+            device_id_type=MESH,
+        )
+
+    def project(a, i):
         acc[...] = jnp.zeros_like(acc)
 
-        def step(kb, carry):
-            cols = pl.ds(pl.multiple_of(kb * CG, CG), CG)
-            acc[...] += dot(lhs_ref[:, cols], w[i, kb].reshape(CG, CG))
+        def step(b, carry):
+            acc[...] += dot(lhs[a, b], w[i, b].reshape(CG, CG))
             return carry
 
-        lax.fori_loop(0, NCTX // NZ, step, 0)
+        lax.fori_loop(0, NX, step, 0)
+        psnd[i] = acc[token_rows(yo), :].astype(BF16)
+        give(i).start()
+        own[i] = acc[token_rows(y), :]
+
+    def rows_in(a):
+        for b in range(NX):
+            pltpu.make_async_copy(
+                (f_ref, g_ref)[a].at[:, columns(b * NY + y)],
+                lhs.at[a, b, token_rows(y)],
+                lsem.at[a, b],
+            ).wait()
+            swap(a, b).wait_recv()
 
     def finish(i):
-        arrive(0, i, 8, 12)
-        arrive(1, i, 11, 12)
-
+        arrive(0, i, 7, 11)
+        arrive(1, i, 10, 11)
+
+    def total(i):
+        give(i).wait_recv()
+        return own[i] + prcv[i].astype(F32)
+
+    rows_in(0)
     finish(0)
-    project(f_ref, 0)
-    value_t = acc[...].T.reshape(NCTX, CB, TOK)
+    project(0, 0)
+    finish(1)
+    project(0, 1)
+    value_t = total(0).T.reshape(NCTX, CB, TOK)
     x32[...] = jnp.concatenate([value_t, value_t], axis=1).reshape(x32.shape)
-    finish(1)
-    project(f_ref, 1)
-    query[...] = acc[...].astype(BF16).astype(F32)
+    rows_in(1)
     finish(2)
-    project(g_ref, 2)
-    gg[...] = acc[...]
-    grad_t = (acc[...] * query[...]).T.reshape(NCTX, CB, TOK)
+    project(1, 2)
+    query[...] = total(1).astype(BF16).astype(F32)
+    gg[...] = total(2)
+    grad_t = (gg[...] * query[...]).T.reshape(NCTX, CB, TOK)
     both = jnp.concatenate([x32[...].reshape(NCTX, 2 * CB, TOK)[:, :CB], grad_t], axis=1)
     snd[...] = both.astype(BF16)
 
@@ -385,55 +431,124 @@
     snd2[...] = y32[...].reshape(snd2.shape).astype(BF16)
     exchange(snd2, rcv2, 1)
 
+    def share(i):
+        return pltpu.make_async_remote_copy(
+            src_ref=pair.at[i, token_rows(y)],
+            dst_ref=pair.at[i, token_rows(y)],
+            send_sem=ysem.at[0, 3 + i],
+            recv_sem=ysem.at[1, 3 + i],
+            device_id=partner,
+            device_id_type=MESH,
+        )
+
+    def shared(i):
+        return pltpu.make_async_remote_copy(
+            src_ref=pair.at[i, token_rows(yo)],
+            dst_ref=pair.at[i, token_rows(yo)],
+            send_sem=ysem.at[0, 3 + i],
+            recv_sem=ysem.at[1, 3 + i],
+            device_id=partner,
+            device_id_type=MESH,
+        )
+
     back = rcv2[...].astype(F32)
     state = back[:, :CB].reshape(CG, TOK).T
-    grad_value = back[:, CB:].reshape(CG, TOK).T.astype(BF16)
-    gated = (query[...] * state).astype(BF16)
-    grad_query = (gg[...] * state).astype(BF16)
+    pair[0, token_rows(y), :] = (query[...] * state).astype(BF16)
+    share(0).start()
+    pair[1, token_rows(y), :] = (gg[...] * state).astype(BF16)
+    share(1).start()
+    pair[2, token_rows(y), :] = back[:, CB:].reshape(CG, TOK).T.astype(BF16)
+    share(2).start()
+
+    def to_sibling(which, b):
+        return pltpu.make_async_remote_copy(
+            src_ref=part.at[which, b],
+            dst_ref=sib.at[which, b],
+            send_sem=csem.at[0, which, b],
+            recv_sem=csem.at[1, which, b],
+            device_id=sibling,
+            device_id_type=MESH,
+        )
+
+    def onward(which, b):
+        return pltpu.make_async_remote_copy(
+            src_ref=summed.at[which, b],
+            dst_ref=got.at[which, y_hi],
+            send_sem=psem.at[0, which, b],
+            recv_sem=psem.at[1, which, y_hi],
+            device_id=(sum_ctx, b * 2 + y),
+            device_id_type=MESH,
+        )
+
+    def at_home(which):
+        return pltpu.make_async_copy(
+            summed.at[which, y_hi], got.at[which, y_hi], psem.at[1, which, y_hi]
+        )
 
     def scatter(which, block):
-        def one(k, carry):
-            to = (tp + k) % NTP
-            part[which, to] = block(to).astype(BF16)
-
-            @pl.when(k < NTP)
+        def give_half(k, carry):
+            b = (y_hi + k) % NX
+            part[which, b] = block(token_rows(1 - core), b).astype(BF16)
+            to_sibling(which, b).start()
+            return carry
+
+        def send_on(k, carry):
+            b = (y_hi + k) % NX
+            mine = block(token_rows(core), b)
+            to_sibling(which, b).wait_recv()
+            summed[which, b] = (mine + sib[which, b].astype(F32)).astype(BF16)
+            home = jnp.logical_and(to_self, b == y_hi)
+
+            @pl.when(home)
             def _():
-                pltpu.make_async_remote_copy(
-                    src_ref=part.at[which, to],
-                    dst_ref=got.at[which, tp],
-                    send_sem=psem.at[which, 0],
-                    recv_sem=psem.at[which, 1],
-                    device_id=(ctx, to),
-                    device_id_type=MESH,
-                ).start()
+                at_home(which).start()
+
+            @pl.when(jnp.logical_not(home))
+            def _():
+                onward(which, b).start()
 
             return carry
 
-        lax.fori_loop(1, NTP + 1, one, 0)
-        got[which, tp] = part[which, tp]
+        lax.fori_loop(1, NX + 1, give_half, 0)
+        lax.fori_loop(1, NX + 1, send_on, 0)
 
     def collect(which, out):
-        rest = got.at[which, pl.ds(0, NTP - 1)]
-        pltpu.make_async_copy(rest, rest, psem.at[which, 1]).wait()
-        total = got[which, 0].astype(F32)
-        for k in range(1, NTP):
-            total += got[which, k].astype(F32)
+        total = None
+        for k in range(NX):
+            pltpu.make_async_copy(got.at[which, k], got.at[which, k], psem.at[1, which, k]).wait()
+            term = got[which, k].astype(F32)
+            total = term if k == 0 else total + term
         out[...] = total.astype(BF16)
 
-    scatter(0, lambda q: dot(gated, w[2, q].reshape(CG, CG), NT))
+    shared(0).wait_recv()
+    scatter(0, lambda rows, b: dot(pair[0, rows, :], w[2, b].reshape(CG, CG), NT))
+    shared(1).wait_recv()
+    shared(2).wait_recv()
     scatter(
         1,
-        lambda q: dot(grad_query, w[1, q].reshape(CG, CG), NT)
-        + dot(grad_value, w[0, q].reshape(CG, CG), NT),
+        lambda rows, b: dot(pair[1, rows, :], w[1, b].reshape(CG, CG), NT)
+        + dot(pair[2, rows, :], w[0, b].reshape(CG, CG), NT),
     )
     collect(0, mixed_ref)
     collect(1, gin_ref)
 
     sent(snd, 0)
     sent(snd2, 1)
+    for a in range(2):
+        for b in range(NX):
+            swap(a, b).wait_send()
+    for i in every:
+        give(i).wait_send()
+        share(i).wait_send()
     for which in range(2):
-        rest = part.at[which, pl.ds(0, NTP - 1)]
-        pltpu.make_async_copy(rest, rest, psem.at[which, 0]).wait()
+        for b in range(NX):
+            to_sibling(which, b).wait_send()
+            home = jnp.logical_and(to_self, b == y_hi)
+
+            @pl.when(jnp.logical_not(home))
+            def _():
+                onward(which, b).wait_send()
+
     for half in range(2):
         for i in every:
             for k in range(NK):
@@ -451,8 +566,12 @@
     )
     vmem = pl.BlockSpec(memory_space=pltpu.VMEM)
     scratch = [
-        pltpu.VMEM((3, NX * NY, NZ, ROWS, CG), BF16),
-        pltpu.VMEM((TOK, CG), F32),
+        pltpu.VMEM((3, NX, NZ, ROWS, CG), BF16),
+        pltpu.VMEM((2, NX, 2 * TOK, CG), BF16),
+        pltpu.VMEM((2 * TOK, CG), F32),
+        pltpu.VMEM((3, TOK, CG), F32),
+        pltpu.VMEM((3, TOK, CG), BF16),
+        pltpu.VMEM((3, TOK, CG), BF16),
         pltpu.VMEM((TOK, CG), F32),
         pltpu.VMEM((TOK, CG), F32),
         pltpu.VMEM((NCTX, 2 * CB, TOK), BF16),
@@ -468,12 +587,19 @@
         pltpu.VMEM((CB, TOK, TOK), BF16),
         pltpu.VMEM((CB, TOK, TOK), BF16),
         pltpu.VMEM((LANES, TOK), F32),
-        pltpu.VMEM((2, NTP, TOK, CG), BF16),
-        pltpu.VMEM((2, NTP, TOK, CG), BF16),
+        pltpu.VMEM((3, 2 * TOK, CG), BF16),
+        pltpu.VMEM((2, NX, TOK, CG), BF16),
+        pltpu.VMEM((2, NX, TOK, CG), BF16),
+        pltpu.VMEM((2, NX, TOK, CG), BF16),
+        pltpu.VMEM((2, NX, TOK, CG), BF16),
         pltpu.SemaphoreType.DMA((2, 3, NK)),
         pltpu.SemaphoreType.DMA((2, 3, NK)),
+        pltpu.SemaphoreType.DMA((2, NX)),
+        pltpu.SemaphoreType.DMA((2, 2, NX)),
+        pltpu.SemaphoreType.DMA((2, 6)),
         pltpu.SemaphoreType.DMA((2, 2)),
-        pltpu.SemaphoreType.DMA((2, 2)),
+        pltpu.SemaphoreType.DMA((2, 2, NX)),
+        pltpu.SemaphoreType.DMA((2, 2, NX)),
     ]
     mixed, grad_in, res = pl.pallas_call(
         kernel,
@@ -482,7 +608,7 @@
             jax.ShapeDtypeStruct((TOK, CG), BF16),
             jax.ShapeDtypeStruct((8, LANES), F32),
         ),
-        in_specs=[vmem] * 6,
+        in_specs=[pl.BlockSpec(memory_space=pl.ANY)] * 2 + [vmem] * 4,
         out_specs=(vmem,) * 3,
         scratch_shapes=scratch,
         compiler_params=pltpu.CompilerParams(

time: 173 us -> 131 us (0.76)
  Pallas kernels: 164 us -> 122 us
    pallas_call x1, Pallas kernels: 164 us -> 122 us  [body(): pl.pallas_call(kernel, out_shape=(jax.ShapeDtypeStruct((TOK, CG), BF16),...]
where the time goes in v2:
time: 131 us; the launch traced here: 130 us
  Pallas kernels  122 us (93%)
  local copies, waits for them, and re-layouts  7.6 us (6%)
    pallas_call x1, Pallas kernels, body(): pl.pallas_call(kernel, out_shape=(jax.ShapeDtypeStruct((TOK, CG), BF16),...  122 us
    unnamed x14, local copies, waits for them, and re-layouts  4.61 us

profile of v2, /device:TPU:1, one launch (start us, length us, event | category | flops | bytes accessed | tf_op | source)
XLA Modules:
  0.0 130.0 jit_solution(179624825120365947)
XLA Ops:
  0.6 0.0 copy-start
  0.7 0.0 copy-start.4
  0.7 0.0 copy-start.3
  0.7 0.8 dynamic_slice.15
  1.5 0.1 broadcast_in_dim.4
  1.5 0.1 reshape.22
  1.6 0.0 copy-done
  1.6 0.1 dynamic-slice_bitcast_fusion.2
  1.7 0.1 copy.12
  1.8 0.1 reshape.19
  1.8 0.8 dynamic-slice_bitcast_fusion
  2.6 0.1 copy.14
  2.7 0.1 reshape.21
  2.8 0.1 copy.13
  2.9 0.1 reshape.20
  3.0 0.0 copy-done.4
  3.0 0.0 copy-done.3
  3.0 0.0 copy-start.1
  3.0 1.2 copy-done.1
  4.2 0.0 copy-start.2
  4.2 1.2 copy-done.2
  5.4 0.0 copy-start.5
  5.5 0.8 copy-done.5
  6.3 121.7 %shard_map.112 = (bf16[128,512]{1,0:T(8,128)(2,1)S(1)}, bf16[128,512]{1,0:T(8,128)(2,1)S(1)}, f32[8,128]{1,0:T(8,128)S(1)}) custom-call(bf16[128,4096]{1,0:T(8,128)(2,1)S(1)} %copy-done.1, bf16[128,4096]{1,0:T(8,128)(2,1)S(1)} %copy-done.2, bf16[64,512]{1,0:T(8,128)(2,1)S(1)} %copy-done.3, bf16[64,512]{1,0:T(8,128)(2,1)S(1)} %copy-done.4, ...), custom_call_target="tpu_custom_call" | custom-call | flops 3221225472 | bytes 4194304 | tf_op jit(solution)/shard_map/pallas_call | solution.py:604
  128.0 0.7 reshape_squeeze.3
  128.7 0.7 copy.17
  129.3 0.7 copy.18
  (3 shorter events, 0.0 us)
Async XLA Ops:
  0.6 1.0 copy-start
  0.7 2.3 %copy-start.4 = (bf16[64,512]{1,0:T(8,128)(2,1)S(1)}, bf16[64,512]{1,0:T(8,128)(2,1)}, u32[]{:S(2)}) copy-start(bf16[64,512]{1,0:T(8,128)(2,1)} %wq_ref.1) | copy-start | bytes 196612
  0.7 2.3 %copy-start.3 = (bf16[64,512]{1,0:T(8,128)(2,1)S(1)}, bf16[64,512]{1,0:T(8,128)(2,1)}, u32[]{:S(2)}) copy-start(bf16[64,512]{1,0:T(8,128)(2,1)} %wv_ref.1) | copy-start | bytes 196612
  3.0 1.2 copy-start.1
  4.2 1.2 copy-start.2
  5.4 0.8 copy-start.5

commit v3 on v2

v3 whole, which is shorter than its diff:
```python
import functools

import jax
import jax.numpy as jnp
from jax import lax
from jax.experimental import pallas as pl
from jax.experimental.pallas import tpu as pltpu
from jax.sharding import PartitionSpec as P

MESH = pl.DeviceIdType.MESH
F32, BF16 = jnp.float32, jnp.bfloat16
NX, NY, NZ = 4, 2, 8
NCTX, NTP = 64, 8
NXZ = NX * NZ
ROWS = 64
HALF = ROWS // 2
CG = 512
TOK = 128
CB = 8
ORDER = 16
LANES = CB * ORDER
NK = 20

NN = (((1,), (0,)), ((), ()))
NT = (((1,), (1,)), ((), ()))


def dot(a, b, dims=NN):
    return lax.dot_general(a, b, dims, preferred_element_type=F32)


def split(a):
    high = a.astype(BF16)
    return high, (a - high.astype(F32)).astype(BF16)


def build_tables(prm_ref, phi, plo, qhi, qlo, thi, tlo, bas):
    prm = prm_ref[...]
    row = lambda k: prm[k : k + 1, :]
    col = lambda k: jnp.broadcast_to(row(k), (LANES, LANES)).T
    d_row, f_row = row(0), row(1)
    d_col, f_col, r_col = col(0), col(1), col(2)
    lane = lax.broadcasted_iota(jnp.int32, (LANES, TOK), 1)
    sub = lax.broadcasted_iota(jnp.int32, (LANES, TOK), 0)
    t_q = (lane + 1).astype(F32)
    t_b = lane.astype(F32)
    t_p = (TOK - 1 - sub).astype(F32)
    mag = jnp.exp(-d_col * t_q)
    ang = f_col * t_q
    q_re, q_im = mag * jnp.cos(ang), mag * jnp.sin(ang)
    basis = jnp.exp(-d_col * t_b) * jnp.cos(f_col * t_b)
    bas[...] = basis
    mag = jnp.exp(-d_row * t_p)
    ang = f_row * t_p
    p_re, p_im = mag * jnp.cos(ang), mag * jnp.sin(ang)
    filt = jnp.sum((r_col * basis).reshape(CB, ORDER, TOK), axis=1)
    for c in range(CB):
        cols = slice(c * TOK, (c + 1) * TOK)
        own = lane // ORDER == c
        high, low = split(
            jnp.concatenate([jnp.where(own, p_re, 0.0), jnp.where(own, p_im, 0.0)], axis=1)
        )
        phi[cols, :] = high
        plo[cols, :] = low
        own = sub // ORDER == c
        high, low = split(
            jnp.concatenate([jnp.where(own, q_re, 0.0), jnp.where(own, q_im, 0.0)], axis=0)
        )
        qhi[:, cols] = high
        qlo[:, cols] = low
        rolled = pltpu.roll(
            jnp.broadcast_to(filt[c : c + 1, :], (TOK, TOK)), 0, 1, stride=1, stride_axis=0
        )
        skip = prm[3:4, c * ORDER : c * ORDER + 1]
        toep = jnp.where(lane >= sub, rolled, 0.0) + jnp.where(lane == sub, skip, 0.0)
        high, low = split(toep)
        thi[c] = high
        tlo[c] = low


def scan_chunks(re, im, lam, forward):
    at = lax.broadcasted_iota(jnp.int32, re.shape, 0)

    def shift(a, by):
        if forward:
            return jnp.where(at >= by, pltpu.roll(a, by, 0), 0.0)
        return jnp.where(at < NCTX - by, pltpu.roll(a, NCTX - by, 0), 0.0)

    re, im = shift(re, 1), shift(im, 1)
    by = 1
    for l_re, l_im in lam:
        s_re, s_im = shift(re, by), shift(im, by)
        re, im = re + l_re * s_re - l_im * s_im, im + l_re * s_im + l_im * s_re
        by *= 2
    return re, im


def chunk_step(prm_ref):
    prm = prm_ref[...]
    d_row, f_row = prm[0:1, :], prm[1:2, :]
    lam = []
    for k in range(6):
        span = float(TOK * 2**k)
        mag = jnp.exp(-d_row * span)
        lam.append((mag * jnp.cos(f_row * span), mag * jnp.sin(f_row * span)))
    return lam, prm[2:3, :]


def channels_of(ref):
    return [ref[pl.ds(c, NCTX, stride=CB), :].astype(BF16) for c in range(CB)]


def convolve(prm_ref, x32, y32, states, phi, plo, qhi, qlo, thi, tlo):
    lam, r_row = chunk_step(prm_ref)
    xs = channels_of(x32)
    xcat = jnp.concatenate(xs, axis=1)
    e = dot(xcat, phi[...]) + dot(xcat, plo[...])
    h_re, h_im = scan_chunks(e[:, :LANES], e[:, LANES:], lam, True)
    states[0] = h_re
    states[1] = h_im
    hh, hl = split(jnp.concatenate([r_row * h_re, -r_row * h_im], axis=1))
    y = dot(hh, qhi[...]) + dot(hl, qhi[...]) + dot(hh, qlo[...])
    for c in range(CB):
        cols = slice(c * TOK, (c + 1) * TOK)
        y32[pl.ds(c, NCTX, stride=CB), :] = y[:, cols] + dot(xs[c], thi[c]) + dot(xs[c], tlo[c])


def convolve_back(prm_ref, g32, z32, phi, plo, qhi, qlo, thi, tlo):
    lam, r_row = chunk_step(prm_ref)
    gs = channels_of(g32)
    gcat = jnp.concatenate(gs, axis=1)
    f = dot(gcat, qhi[...], NT) + dot(gcat, qlo[...], NT)
    k_re, k_im = scan_chunks(f[:, :LANES], f[:, LANES:], lam, False)
    kh, kl = split(jnp.concatenate([r_row * k_re, -r_row * k_im], axis=1))
    z = dot(kh, phi[...], NT) + dot(kl, phi[...], NT) + dot(kh, plo[...], NT)
    for c in range(CB):
        cols = slice(c * TOK, (c + 1) * TOK)
        z32[pl.ds(c, NCTX, stride=CB), :] = (
            z[:, cols] + dot(gs[c], thi[c], NT) + dot(gs[c], tlo[c], NT)
        )
    return gs, f


def amplitudes(x32, gs, f, states, bas, res_ref):
    across = jnp.sum(states[0] * f[:, :LANES] - states[1] * f[:, LANES:], axis=0, keepdims=True)
    lane = lax.broadcasted_iota(jnp.int32, (TOK, TOK), 1)
    sub = lax.broadcasted_iota(jnp.int32, (TOK, TOK), 0)
    flip = jnp.where(lane + sub == TOK - 1, 1.0, 0.0).astype(BF16)
    xs = channels_of(x32)
    corr = []
    for c in range(CB):
        back_t = dot(xs[c], flip).T.astype(BF16)
        pairs = dot(back_t, gs[c])
        lagged = pltpu.roll(pairs, 1, 1, stride=1, stride_axis=0)
        corr.append(jnp.sum(jnp.where(lane <= sub, lagged, 0.0), axis=0, keepdims=True))
    spread = jnp.concatenate([jnp.broadcast_to(a, (ORDER, TOK)) for a in corr], axis=0)
    within = jnp.sum((spread * bas[...]).T, axis=0, keepdims=True)
    res_ref[...] = jnp.broadcast_to(within + across, res_ref.shape)


def kernel(
    f_ref,
    g_ref,
    wv_ref,
    wq_ref,
    wo_ref,
    prm_ref,
    mixed_ref,
    gin_ref,
    res_ref,
    w,
    lhs,
    acc,
    turned,
    psnd,
    prcv,
    query,
    gg,
    state,
    snd,
    rcv,
    x32,
    g32,
    y32,
    states,
    phi,
    plo,
    qhi,
    qlo,
    thi,
    tlo,
    bas,
    pair,
    gat,
    part,
    sib,
    summed,
    got,
    ssem,
    rsem,
    lsem,
    fsem,
    ysem,
    xsem,
    csem,
    psem,
):
    ctx = lax.axis_index("ctx")
    tp = lax.axis_index("tp")
    xy = ctx // NZ
    x, y, z = xy // NY, xy % NY, ctx % NZ
    y_hi, core = tp // 2, tp % 2
    xl, xr, x2 = (x + NX - 1) % NX, (x + 1) % NX, (x + 2) % NX
    zl, zr = (z + NZ - 1) % NZ, (z + 1) % NZ
    yo = 1 - y
    at = lambda xi, yi, zi: (xi * NY + yi) * NZ + zi
    partner = (at(x, yo, z), tp)
    sibling = (ctx, y_hi * 2 + 1 - core)
    sum_ctx = at(x, core, z)
    to_self = core == y

    barrier = pltpu.get_barrier_semaphore()

    def greet(device):
        pl.semaphore_signal(barrier, inc=1, device_id=device, device_id_type=MESH)

    lane_of = x * NZ + z

    def mate(k):
        to = (lane_of + k) % NXZ
        return to, (at(to // NZ, y, to % NZ), tp)

    def greet_mate(k, carry):
        greet(mate(k)[1])
        return carry

    lax.fori_loop(1, NXZ, greet_mate, 0)
    greet(partner)
    greet(sibling)
    for k in range(1, NX):
        greet((sum_ctx, (y_hi + k) % NX * 2 + y))

    @pl.when(jnp.logical_not(to_self))
    def _():
        greet((sum_ctx, y_hi * 2 + y))

    def columns(block):
        return pl.ds(pl.multiple_of(block * CG, CG), CG)

    def token_rows(yi):
        return pl.ds(pl.multiple_of(yi * TOK, TOK), TOK)

    for i, ref in enumerate((wv_ref, wq_ref, wo_ref)):
        w[i, x, z] = ref[...]
    for a, ref in enumerate((f_ref, g_ref)):
        for b in range(NX):
            pltpu.make_async_copy(
                ref.at[:, columns(b * NY + y)], lhs.at[a, b, token_rows(y)], lsem.at[a, b]
            ).start()
    pl.semaphore_wait(barrier, NXZ - 1 + 2 + NX - 1 + jnp.where(to_self, 0, 1))

    def swap(a, b):
        return pltpu.make_async_remote_copy(
            src_ref=(f_ref, g_ref)[a].at[:, columns(b * NY + yo)],
            dst_ref=lhs.at[a, b, token_rows(y)],
            send_sem=fsem.at[0, a, b],
            recv_sem=fsem.at[1, a, b],
            device_id=partner,
            device_id_type=MESH,
        )

    for a in range(2):
        for b in range(NX):
            swap(a, b).start()

    def copy(half, i, k, ref, device):
        return pltpu.make_async_remote_copy(
            src_ref=ref,
            dst_ref=ref,
            send_sem=ssem.at[half, i, k],
            recv_sem=rsem.at[half, i, k],
            device_id=device,
            device_id_type=MESH,
        )

    to_r, to_l = (at(xr, y, z), tp), (at(xl, y, z), tp)
    to_u, to_d = (at(x, y, zr), tp), (at(x, y, zl), tp)
    quarter = HALF // 2
    first, second = pl.ds(0, HALF), pl.ds(HALF, HALF)

    def z_from(step, up):
        return (z + NZ - step) % NZ if up else (z + step) % NZ

    def a_copy(i, k):
        if k < 2:
            return w.at[i, x, z, first], (to_r, to_l)[k], w.at[i, (xl, xr)[k], z, first]
        if k < 4:
            rows = pl.ds((k - 2) * quarter, quarter)
            return w.at[i, (xl, xr)[k - 2], z, rows], (to_r, to_l)[k - 2], w.at[i, x2, z, rows]
        step, up, some = (k - 4) // 4, (k - 4) // 2 % 2 == 0, pl.ds(k % 2 * (NX // 2), NX // 2)
        return (
            w.at[i, some, z_from(step, up), first],
            to_u if up else to_d,
            w.at[i, some, z_from(step + 1, up), first],
        )

    def b_copy(i, k):
        if k < 8:
            up, step = k < 4, k % 4
            rows = second if step < 3 else pl.ds(HALF if up else HALF + quarter, quarter)
            return (
                w.at[i, x, z_from(step, up), rows],
                to_u if up else to_d,
                w.at[i, x, z_from(step + 1, up), rows],
            )
        if k < 12:
            way, some = (k - 8) // 2, pl.ds(k % 2 * (NZ // 2), NZ // 2)
            return (
                w.at[i, x, some, second],
                (to_r, to_l)[way],
                w.at[i, (xl, xr)[way], some, second],
            )
        way, some = k - 12, pl.ds((k - 12) * (NZ // 2), NZ // 2)
        return w.at[i, (xl, xr)[way], some, second], (to_r, to_l)[way], w.at[i, x2, some, second]

    used = (tuple(range(16)) + (16, 19), tuple(range(14)))
    makers = (a_copy, b_copy)

    def start(half, i, *ks):
        for k in ks:
            out, device, _ = makers[half](i, k)
            copy(half, i, k, out, device).start()

    def arrive(half, i, *ks):
        for k in ks:
            _, device, incoming = makers[half](i, k)
            copy(half, i, k, incoming, device).wait_recv()

    every = range(3)

    def a_start(i):
        arrive(0, i, 2, 3)
        start(0, i, 4, 6, 5, 7)

    def a_next(i, step):
        k = 4 + 4 * step
        for one in (k, k + 3, k + 1, k + 2):
            arrive(0, i, one)
            if one + 4 in used[0]:
                start(0, i, one + 4)

    def b_start(i):
        arrive(1, i, 3, 7)
        start(1, i, 8, 11, 9, 10)

    def b_second(i):
        arrive(1, i, 8)
        start(1, i, 12)
        arrive(1, i, 11)
        start(1, i, 13)

    def finish(i):
        arrive(0, i, 16, 19)
        arrive(1, i, 9, 10, 12, 13)

    def give(i):
        return pltpu.make_async_remote_copy(
            src_ref=psnd.at[i],
            dst_ref=prcv.at[i],
            send_sem=ysem.at[0, i],
            recv_sem=ysem.at[1, i],
            device_id=partner,
            device_id_type=MESH,
        )

    def project(a, i):
        acc[...] = jnp.zeros_like(acc)

        def step(b, carry):
            acc[...] += dot(lhs[a, b], w[i, b].reshape(CG, CG))
            return carry

        lax.fori_loop(0, NX, step, 0)
        turned[i] = acc[...].T.reshape(turned.shape[1:])
        psnd[i] = turned[i, :, yo].astype(BF16)
        give(i).start()

    def rows_in(a):
        for b in range(NX):
            pltpu.make_async_copy(
                (f_ref, g_ref)[a].at[:, columns(b * NY + y)],
                lhs.at[a, b, token_rows(y)],
                lsem.at[a, b],
            ).wait()
            swap(a, b).wait_recv()

    def total(i):
        give(i).wait_recv()
        return turned[i, :, y] + prcv[i].astype(F32)

    def exchange(which):
        def one(k, carry):
            to, device = mate(k)
            pltpu.make_async_remote_copy(
                src_ref=snd.at[which, to],
                dst_ref=rcv.at[which, lane_of],
                send_sem=xsem.at[which, 0],
                recv_sem=xsem.at[which, 1],
                device_id=device,
                device_id_type=MESH,
            ).start()
            return carry

        lax.fori_loop(1, NXZ, one, 0)
        rcv[which, lane_of] = snd[which, lane_of]

    def exchanged(which):
        rest = rcv.at[which, pl.ds(0, NXZ - 1)]
        pltpu.make_async_copy(rest, rest, xsem.at[which, 1]).wait()

    def to_chunks(which, a):
        a = a.reshape(NXZ, CB, 2 * TOK)
        snd[which] = jnp.concatenate([a[:, :, :TOK], a[:, :, TOK:]], axis=1).astype(BF16)

    def from_chunks(which):
        a = rcv[which].astype(F32)
        return jnp.concatenate([a[:, :CB], a[:, CB:]], axis=2).reshape(NX, ROWS, 2 * TOK)

    def chunks_in(which, ref):
        for xi in range(NX):
            a = rcv[which, xi * NZ : (xi + 1) * NZ].astype(F32)
            for yi in range(NY):
                at_row = (xi * NY + yi) * ROWS
                ref[at_row : at_row + ROWS, :] = a[:, yi * CB : (yi + 1) * CB].reshape(ROWS, TOK)

    def chunks_out(which):
        for xi in range(NX):
            both = [
                y32[(xi * NY + yi) * ROWS : (xi * NY + yi + 1) * ROWS, :].reshape(NZ, CB, TOK)
                for yi in range(NY)
            ]
            snd[which, xi * NZ : (xi + 1) * NZ] = jnp.concatenate(both, axis=1).astype(BF16)

    def share(i, yi):
        return pltpu.make_async_remote_copy(
            src_ref=pair.at[i, :, yi],
            dst_ref=pair.at[i, :, yi],
            send_sem=ysem.at[0, 3 + i],
            recv_sem=ysem.at[1, 3 + i],
            device_id=partner,
            device_id_type=MESH,
        )

    def put(i, a):
        pair[i, :, y] = a.astype(BF16)
        share(i, y).start()

    def shared(i):
        share(i, yo).wait_recv()
        gat[i] = pair[i].astype(F32).reshape(CG, 2 * TOK).T.astype(BF16)

    def to_sibling(which, b):
        return pltpu.make_async_remote_copy(
            src_ref=part.at[which, b],
            dst_ref=sib.at[which, b],
            send_sem=csem.at[0, which, b],
            recv_sem=csem.at[1, which, b],
            device_id=sibling,
            device_id_type=MESH,
        )

    def onward(which, b):
        return pltpu.make_async_remote_copy(
            src_ref=summed.at[which, b],
            dst_ref=got.at[which, y_hi],
            send_sem=psem.at[0, which, b],
            recv_sem=psem.at[1, which, y_hi],
            device_id=(sum_ctx, b * 2 + y),
            device_id_type=MESH,
        )

    def at_home(which):
        return pltpu.make_async_copy(
            summed.at[which, y_hi], got.at[which, y_hi], psem.at[1, which, y_hi]
        )

    def scatter(which, block):
        def give_half(k, carry):
            b = (y_hi + k) % NX
            part[which, b] = block(token_rows(1 - core), b).astype(BF16)
            to_sibling(which, b).start()
            return carry

        def send_on(k, carry):
            b = (y_hi + k) % NX
            mine = block(token_rows(core), b)
            to_sibling(which, b).wait_recv()
            summed[which, b] = (mine + sib[which, b].astype(F32)).astype(BF16)
            home = jnp.logical_and(to_self, b == y_hi)

            @pl.when(home)
            def _():
                at_home(which).start()

            @pl.when(jnp.logical_not(home))
            def _():
                onward(which, b).start()

            return carry

        lax.fori_loop(1, NX + 1, give_half, 0)
        lax.fori_loop(1, NX + 1, send_on, 0)

    def collect(which, out):
        total = None
        for k in range(NX):
            pltpu.make_async_copy(got.at[which, k], got.at[which, k], psem.at[1, which, k]).wait()
            term = got[which, k].astype(F32)
            total = term if k == 0 else total + term
        out[...] = total.astype(BF16)

    for i in every:
        start(0, i, 0, 1)
        start(1, i, 0, 4)
    for i in every:
        arrive(0, i, 0)
        start(0, i, 2)
        arrive(0, i, 1)
        start(0, i, 3)
        arrive(1, i, 0, 4)
        start(1, i, 1, 5)
    a_start(0)
    for i in every:
        arrive(1, i, 1, 5)
        start(1, i, 2, 6)
    for i in every:
        arrive(1, i, 2, 6)
        start(1, i, 3, 7)
    b_start(0)
    a_next(0, 0)
    a_start(1)
    a_next(0, 1)
    b_second(0)
    b_start(1)
    a_next(0, 2)
    a_next(1, 0)
    a_start(2)
    rows_in(0)
    finish(0)
    project(0, 0)
    a_next(1, 1)
    b_second(1)
    b_start(2)
    build_tables(prm_ref, phi, plo, qhi, qlo, thi, tlo, bas)
    to_chunks(0, total(0))
    exchange(0)
    a_next(2, 0)
    a_next(1, 2)
    exchanged(0)
    chunks_in(0, x32)
    convolve(prm_ref, x32, y32, states, phi, plo, qhi, qlo, thi, tlo)
    chunks_out(1)
    exchange(1)
    a_next(2, 1)
    b_second(2)
    finish(1)
    project(0, 1)
    a_next(2, 2)
    exchanged(1)
    state[...] = from_chunks(1)
    query[...] = total(1).astype(BF16).astype(F32)
    put(0, query[...] * state[...])
    rows_in(1)
    finish(2)
    project(1, 2)
    gg[...] = total(2)
    to_chunks(2, gg[...] * query[...])
    exchange(2)
    put(1, gg[...] * state[...])
    shared(0)
    scatter(0, lambda rows, b: dot(gat[0, rows, :], w[2, b].reshape(CG, CG), NT))
    exchanged(2)
    chunks_in(2, g32)
    gs, f = convolve_back(prm_ref, g32, y32, phi, plo, qhi, qlo, thi, tlo)
    chunks_out(3)
    exchange(3)
    amplitudes(x32, gs, f, states, bas, res_ref)
    shared(1)
    collect(0, mixed_ref)
    exchanged(3)
    put(2, from_chunks(3))
    shared(2)
    scatter(
        1,
        lambda rows, b: dot(gat[1, rows, :], w[1, b].reshape(CG, CG), NT)
        + dot(gat[2, rows, :], w[0, b].reshape(CG, CG), NT),
    )
    collect(1, gin_ref)

    for which in range(4):
        rest = snd.at[which, pl.ds(0, NXZ - 1)]
        pltpu.make_async_copy(rest, rest, xsem.at[which, 0]).wait()
    for a in range(2):
        for b in range(NX):
            swap(a, b).wait_send()
    for i in every:
        give(i).wait_send()
        share(i, y).wait_send()
    for which in range(2):
        for b in range(NX):
            to_sibling(which, b).wait_send()
            home = jnp.logical_and(to_self, b == y_hi)

            @pl.when(jnp.logical_not(home))
            def _():
                onward(which, b).wait_send()

    for half in range(2):
        for i in every:
            for k in used[half]:
                out, device, _ = makers[half](i, k)
                copy(half, i, k, out, device).wait_send()


def body(features, grad_out, w_value, w_query, w_out, residues, decays, freqs, skips):
    first = lax.axis_index("ctx") * CB
    own = lambda a: lax.dynamic_slice_in_dim(a, first, CB, a.ndim - 1)
    flat = lambda a: own(a).T.reshape(1, LANES)
    skip_row = jnp.broadcast_to(own(skips)[:, None], (CB, ORDER)).reshape(1, LANES)
    prm = jnp.concatenate(
        [flat(decays), flat(freqs), flat(residues), skip_row, jnp.zeros((4, LANES), F32)], axis=0
    )
    vmem = pl.BlockSpec(memory_space=pltpu.VMEM)
    scratch = [
        pltpu.VMEM((3, NX, NZ, ROWS, CG), BF16),
        pltpu.VMEM((2, NX, 2 * TOK, CG), BF16),
        pltpu.VMEM((2 * TOK, CG), F32),
        pltpu.VMEM((3, NX, NY, ROWS, 2 * TOK), F32),
        pltpu.VMEM((3, NX, ROWS, 2 * TOK), BF16),
        pltpu.VMEM((3, NX, ROWS, 2 * TOK), BF16),
        pltpu.VMEM((NX, ROWS, 2 * TOK), F32),
        pltpu.VMEM((NX, ROWS, 2 * TOK), F32),
        pltpu.VMEM((NX, ROWS, 2 * TOK), F32),
        pltpu.VMEM((4, NXZ, 2 * CB, TOK), BF16),
        pltpu.VMEM((4, NXZ, 2 * CB, TOK), BF16),
        pltpu.VMEM((NCTX * CB, TOK), F32),
        pltpu.VMEM((NCTX * CB, TOK), F32),
        pltpu.VMEM((NCTX * CB, TOK), F32),
        pltpu.VMEM((2, NCTX, LANES), F32),
        pltpu.VMEM((CB * TOK, 2 * LANES), BF16),
        pltpu.VMEM((CB * TOK, 2 * LANES), BF16),
        pltpu.VMEM((2 * LANES, CB * TOK), BF16),
        pltpu.VMEM((2 * LANES, CB * TOK), BF16),
        pltpu.VMEM((CB, TOK, TOK), BF16),
        pltpu.VMEM((CB, TOK, TOK), BF16),
        pltpu.VMEM((LANES, TOK), F32),
        pltpu.VMEM((3, NX, NY, ROWS, 2 * TOK), BF16),
        pltpu.VMEM((3, 2 * TOK, CG), BF16),
        pltpu.VMEM((2, NX, TOK, CG), BF16),
        pltpu.VMEM((2, NX, TOK, CG), BF16),
        pltpu.VMEM((2, NX, TOK, CG), BF16),
        pltpu.VMEM((2, NX, TOK, CG), BF16),
        pltpu.SemaphoreType.DMA((2, 3, NK)),
        pltpu.SemaphoreType.DMA((2, 3, NK)),
        pltpu.SemaphoreType.DMA((2, NX)),
        pltpu.SemaphoreType.DMA((2, 2, NX)),
        pltpu.SemaphoreType.DMA((2, 6)),
        pltpu.SemaphoreType.DMA((4, 2)),
        pltpu.SemaphoreType.DMA((2, 2, NX)),
        pltpu.SemaphoreType.DMA((2, 2, NX)),
    ]
    mixed, grad_in, res = pl.pallas_call(
        kernel,
        out_shape=(
            jax.ShapeDtypeStruct((TOK, CG), BF16),
            jax.ShapeDtypeStruct((TOK, CG), BF16),
            jax.ShapeDtypeStruct((8, LANES), F32),
        ),
        in_specs=[pl.BlockSpec(memory_space=pl.ANY)] * 2 + [vmem] * 4,
        out_specs=(vmem,) * 3,
        scratch_shapes=scratch,
        compiler_params=pltpu.CompilerParams(
            collective_id=0, has_side_effects=True, vmem_limit_bytes=48 * 2**20
        ),
        cost_estimate=pl.CostEstimate(
            flops=2 * 6 * TOK * CG * 4096, bytes_accessed=2**22, transcendentals=2**17
        ),
    )(features, grad_out, w_value, w_query, w_out.T, prm)
    return mixed, grad_in, res[0].reshape(CB, ORDER).T


def solution(mesh):
    placed = (
        P("ctx", None),
        P("ctx", None),
        P("ctx", "tp"),
        P("ctx", "tp"),
        P("tp", "ctx"),
        P(None, "tp"),
        P(None, "tp"),
        P(None, "tp"),
        P("tp"),
    )
    return jax.shard_map(
        body,
        mesh=mesh,
        in_specs=placed,
        out_specs=(P("ctx", "tp"), P("ctx", "tp"), P(None, ("tp", "ctx"))),
        check_vma=False,
    )
```

time: 131 us -> 123 us (0.939)
  Pallas kernels: 122 us -> 115 us
    pallas_call x1, Pallas kernels: 122 us -> 115 us  [body(): pl.pallas_call(kernel, out_shape=(jax.ShapeDtypeStruct((TOK, CG), BF16),...]
where the time goes in v3:
time: 123 us
  Pallas kernels  115 us (93%)
  local copies, waits for them, and re-layouts  7.6 us (6%)
    pallas_call x1, Pallas kernels, body(): pl.pallas_call(kernel, out_shape=(jax.ShapeDtypeStruct((TOK, CG), BF16),...  115 us
    unnamed x14, local copies, waits for them, and re-layouts  4.61 us

profile of v3, /device:TPU:1, one launch (start us, length us, event | category | flops | bytes accessed | tf_op | source)
XLA Modules:
  0.0 122.8 jit_solution(15859908636938622374)
XLA Ops:
  0.6 0.0 copy-start
  0.7 0.0 copy-start.4
  0.7 0.0 copy-start.3
  0.7 0.8 dynamic_slice.15
  1.5 0.1 broadcast_in_dim.4
  1.5 0.1 reshape.22
  1.6 0.0 copy-done
  1.6 0.1 dynamic-slice_bitcast_fusion.2
  1.7 0.1 copy.12
  1.8 0.1 reshape.19
  1.8 0.8 dynamic-slice_bitcast_fusion
  2.6 0.1 copy.14
  2.7 0.1 reshape.21
  2.8 0.1 copy.13
  2.9 0.1 reshape.20
  3.0 0.0 copy-done.4
  3.0 0.0 copy-done.3
  3.0 0.0 copy-start.1
  3.0 1.2 copy-done.1
  4.2 0.0 copy-start.2
  4.2 1.2 copy-done.2
  5.4 0.0 copy-start.5
  5.5 0.8 copy-done.5
  6.3 114.5 %shard_map.112 = (bf16[128,512]{1,0:T(8,128)(2,1)S(1)}, bf16[128,512]{1,0:T(8,128)(2,1)S(1)}, f32[8,128]{1,0:T(8,128)S(1)}) custom-call(bf16[128,4096]{1,0:T(8,128)(2,1)S(1)} %copy-done.1, bf16[128,4096]{1,0:T(8,128)(2,1)S(1)} %copy-done.2, bf16[64,512]{1,0:T(8,128)(2,1)S(1)} %copy-done.3, bf16[64,512]{1,0:T(8,128)(2,1)S(1)} %copy-done.4, ...), custom_call_target="tpu_custom_call" | custom-call | flops 3221225472 | bytes 4194304 | tf_op jit(solution)/shard_map/pallas_call | solution.py:672
  120.8 0.7 reshape_squeeze.3
  121.5 0.7 copy.17
  122.2 0.7 copy.18
  (3 shorter events, 0.0 us)
Async XLA Ops:
  0.6 1.0 copy-start
  0.7 2.3 %copy-start.4 = (bf16[64,512]{1,0:T(8,128)(2,1)S(1)}, bf16[64,512]{1,0:T(8,128)(2,1)}, u32[]{:S(2)}) copy-start(bf16[64,512]{1,0:T(8,128)(2,1)} %wq_ref.1) | copy-start | bytes 196612
  0.7 2.3 %copy-start.3 = (bf16[64,512]{1,0:T(8,128)(2,1)S(1)}, bf16[64,512]{1,0:T(8,128)(2,1)}, u32[]{:S(2)}) copy-start(bf16[64,512]{1,0:T(8,128)(2,1)} %wv_ref.1) | copy-start | bytes 196612
  3.0 1.2 copy-start.1
  4.2 1.2 copy-start.2
  5.4 0.8 copy-start.5

commit v4 on v3

--- a/solution.py
+++ b/solution.py
@@ -95,6 +95,21 @@
     return re, im
 
 
+def pick_parameters(raw, skip, ctx, prm):
+    every = jnp.concatenate([raw[...], jnp.broadcast_to(skip[...], (ORDER, CG))], axis=0)
+    high, low = split(every)
+    rest = (every - high.astype(F32) - low.astype(F32)).astype(BF16)
+    channel = lax.broadcasted_iota(jnp.int32, (CG, LANES), 0)
+    lane = lax.broadcasted_iota(jnp.int32, (CG, LANES), 1)
+    one_hot = jnp.where(channel == ctx * CB + lane // ORDER, 1.0, 0.0).astype(BF16)
+    spread = dot(high, one_hot) + dot(low, one_hot) + dot(rest, one_hot)
+    mode = lax.broadcasted_iota(jnp.int32, (ORDER, LANES), 0)
+    own = mode == lax.broadcasted_iota(jnp.int32, (ORDER, LANES), 1) % ORDER
+    for k in range(4):
+        rows = spread[k * ORDER : (k + 1) * ORDER, :]
+        prm[k : k + 1, :] = jnp.sum(jnp.where(own, rows, 0.0), axis=0, keepdims=True)
+
+
 def chunk_step(prm_ref):
     prm = prm_ref[...]
     d_row, f_row = prm[0:1, :], prm[1:2, :]
@@ -164,10 +179,16 @@
     wv_ref,
     wq_ref,
     wo_ref,
-    prm_ref,
+    decay_ref,
+    freq_ref,
+    amp_ref,
+    skip_ref,
     mixed_ref,
     gin_ref,
     res_ref,
+    raw,
+    skip,
+    prm_ref,
     w,
     lhs,
     acc,
@@ -192,12 +213,14 @@
     bas,
     pair,
     gat,
+    pre,
     part,
     sib,
     summed,
     got,
     ssem,
     rsem,
+    gsem,
     lsem,
     fsem,
     ysem,
@@ -250,13 +273,24 @@
     def token_rows(yi):
         return pl.ds(pl.multiple_of(yi * TOK, TOK), TOK)
 
-    for i, ref in enumerate((wv_ref, wq_ref, wo_ref)):
-        w[i, x, z] = ref[...]
+    loads = [
+        pltpu.make_async_copy(ref, w.at[i, x, z], gsem.at[i])
+        for i, ref in enumerate((wv_ref, wq_ref, wo_ref))
+    ]
+    loads += [
+        pltpu.make_async_copy(ref, raw.at[pl.ds(k * ORDER, ORDER)], gsem.at[3 + k])
+        for k, ref in enumerate((decay_ref, freq_ref, amp_ref))
+    ]
+    loads.append(pltpu.make_async_copy(skip_ref, skip, gsem.at[6]))
+    for one in loads:
+        one.start()
     for a, ref in enumerate((f_ref, g_ref)):
         for b in range(NX):
             pltpu.make_async_copy(
                 ref.at[:, columns(b * NY + y)], lhs.at[a, b, token_rows(y)], lsem.at[a, b]
             ).start()
+    for one in loads:
+        one.wait()
     pl.semaphore_wait(barrier, NXZ - 1 + 2 + NX - 1 + jnp.where(to_self, 0, 1))
 
     def swap(a, b):
@@ -363,27 +397,32 @@
         arrive(0, i, 16, 19)
         arrive(1, i, 9, 10, 12, 13)
 
-    def give(i):
+    def give(i, part):
+        some = pl.ds(part * (NX // 2), NX // 2)
         return pltpu.make_async_remote_copy(
-            src_ref=psnd.at[i],
-            dst_ref=prcv.at[i],
-            send_sem=ysem.at[0, i],
-            recv_sem=ysem.at[1, i],
+            src_ref=psnd.at[i, some],
+            dst_ref=prcv.at[i, some],
+            send_sem=ysem.at[0, 2 * i + part],
+            recv_sem=ysem.at[1, 2 * i + part],
             device_id=partner,
             device_id_type=MESH,
         )
 
     def project(a, i):
-        acc[...] = jnp.zeros_like(acc)
-
-        def step(b, carry):
-            acc[...] += dot(lhs[a, b], w[i, b].reshape(CG, CG))
-            return carry
-
-        lax.fori_loop(0, NX, step, 0)
-        turned[i] = acc[...].T.reshape(turned.shape[1:])
-        psnd[i] = turned[i, :, yo].astype(BF16)
-        give(i).start()
+        wide = CG // 2
+        for part in range(2):
+            acc[...] = jnp.zeros_like(acc)
+
+            def step(b, carry):
+                cols = w[i, b, :, :, part * wide : (part + 1) * wide].reshape(CG, wide)
+                acc[...] += dot(lhs[a, b], cols)
+                return carry
+
+            lax.fori_loop(0, NX, step, 0)
+            some = slice(part * (NX // 2), (part + 1) * (NX // 2))
+            turned[i, some] = acc[...].T.reshape(NX // 2, NY, ROWS, 2 * TOK)
+            psnd[i, some] = turned[i, some, yo].astype(BF16)
+            give(i, part).start()
 
     def rows_in(a):
         for b in range(NX):
@@ -395,7 +434,8 @@
             swap(a, b).wait_recv()
 
     def total(i):
-        give(i).wait_recv()
+        give(i, 0).wait_recv()
+        give(i, 1).wait_recv()
         return turned[i, :, y] + prcv[i].astype(F32)
 
     def exchange(which):
@@ -445,8 +485,8 @@
         return pltpu.make_async_remote_copy(
             src_ref=pair.at[i, :, yi],
             dst_ref=pair.at[i, :, yi],
-            send_sem=ysem.at[0, 3 + i],
-            recv_sem=ysem.at[1, 3 + i],
+            send_sem=ysem.at[0, 6 + i],
+            recv_sem=ysem.at[1, 6 + i],
             device_id=partner,
             device_id_type=MESH,
         )
@@ -485,31 +525,42 @@
         )
 
     def scatter(which, block):
-        def give_half(k, carry):
+        def give_half(k):
             b = (y_hi + k) % NX
-            part[which, b] = block(token_rows(1 - core), b).astype(BF16)
+            part[which, b] = block(0, b).astype(BF16)
             to_sibling(which, b).start()
-            return carry
-
-        def send_on(k, carry):
+
+        def send_on(k):
             b = (y_hi + k) % NX
-            mine = block(token_rows(core), b)
+            mine = block(1, b)
             to_sibling(which, b).wait_recv()
             summed[which, b] = (mine + sib[which, b].astype(F32)).astype(BF16)
-            home = jnp.logical_and(to_self, b == y_hi)
-
-            @pl.when(home)
-            def _():
-                at_home(which).start()
-
-            @pl.when(jnp.logical_not(home))
-            def _():
+            if k == NX:
+                home = jnp.logical_and(to_self, b == y_hi)
+
+                @pl.when(home)
+                def _():
+                    at_home(which).start()
+
+                @pl.when(jnp.logical_not(home))
+                def _():
+                    onward(which, b).start()
+            else:
                 onward(which, b).start()
 
-            return carry
-
-        lax.fori_loop(1, NX + 1, give_half, 0)
-        lax.fori_loop(1, NX + 1, send_on, 0)
+        order = (2, 1, 3, 4)
+        give_half(order[0])
+        for k in range(NX):
+            if k + 1 < NX:
+                give_half(order[k + 1])
+            send_on(order[k])
+
+    halves = (token_rows(1 - core), token_rows(core))
+
+    def early(b, carry):
+        for k in range(2):
+            pre[k, b] = dot(gat[1, halves[k], :], w[1, b].reshape(CG, CG), NT)
+        return carry
 
     def collect(which, out):
         total = None
@@ -551,6 +602,7 @@
     a_next(1, 1)
     b_second(1)
     b_start(2)
+    pick_parameters(raw, skip, ctx, prm_ref)
     build_tables(prm_ref, phi, plo, qhi, qlo, thi, tlo, bas)
     to_chunks(0, total(0))
     exchange(0)
@@ -573,28 +625,25 @@
     rows_in(1)
     finish(2)
     project(1, 2)
+    shared(0)
     gg[...] = total(2)
     to_chunks(2, gg[...] * query[...])
     exchange(2)
     put(1, gg[...] * state[...])
-    shared(0)
-    scatter(0, lambda rows, b: dot(gat[0, rows, :], w[2, b].reshape(CG, CG), NT))
+    scatter(0, lambda k, b: dot(gat[0, halves[k], :], w[2, b].reshape(CG, CG), NT))
     exchanged(2)
     chunks_in(2, g32)
     gs, f = convolve_back(prm_ref, g32, y32, phi, plo, qhi, qlo, thi, tlo)
     chunks_out(3)
     exchange(3)
+    shared(1)
+    lax.fori_loop(0, NX, early, 0)
     amplitudes(x32, gs, f, states, bas, res_ref)
-    shared(1)
-    collect(0, mixed_ref)
     exchanged(3)
     put(2, from_chunks(3))
     shared(2)
-    scatter(
-        1,
-        lambda rows, b: dot(gat[1, rows, :], w[1, b].reshape(CG, CG), NT)
-        + dot(gat[2, rows, :], w[0, b].reshape(CG, CG), NT),
-    )
+    scatter(1, lambda k, b: pre[k, b] + dot(gat[2, halves[k], :], w[0, b].reshape(CG, CG), NT))
+    collect(0, mixed_ref)
     collect(1, gin_ref)
 
     for which in range(4):
@@ -604,7 +653,8 @@
         for b in range(NX):
             swap(a, b).wait_send()
     for i in every:
-        give(i).wait_send()
+        give(i, 0).wait_send()
+        give(i, 1).wait_send()
         share(i, y).wait_send()
     for which in range(2):
         for b in range(NX):
@@ -623,18 +673,14 @@
 
 
 def body(features, grad_out, w_value, w_query, w_out, residues, decays, freqs, skips):
-    first = lax.axis_index("ctx") * CB
-    own = lambda a: lax.dynamic_slice_in_dim(a, first, CB, a.ndim - 1)
-    flat = lambda a: own(a).T.reshape(1, LANES)
-    skip_row = jnp.broadcast_to(own(skips)[:, None], (CB, ORDER)).reshape(1, LANES)
-    prm = jnp.concatenate(
-        [flat(decays), flat(freqs), flat(residues), skip_row, jnp.zeros((4, LANES), F32)], axis=0
-    )
     vmem = pl.BlockSpec(memory_space=pltpu.VMEM)
     scratch = [
+        pltpu.VMEM((3 * ORDER, CG), F32),
+        pltpu.VMEM((1, CG), F32),
+        pltpu.VMEM((8, LANES), F32),
         pltpu.VMEM((3, NX, NZ, ROWS, CG), BF16),
         pltpu.VMEM((2, NX, 2 * TOK, CG), BF16),
-        pltpu.VMEM((2 * TOK, CG), F32),
+        pltpu.VMEM((2 * TOK, CG // 2), F32),
         pltpu.VMEM((3, NX, NY, ROWS, 2 * TOK), F32),
         pltpu.VMEM((3, NX, ROWS, 2 * TOK), BF16),
         pltpu.VMEM((3, NX, ROWS, 2 * TOK), BF16),
@@ -656,15 +702,17 @@
         pltpu.VMEM((LANES, TOK), F32),
         pltpu.VMEM((3, NX, NY, ROWS, 2 * TOK), BF16),
         pltpu.VMEM((3, 2 * TOK, CG), BF16),
+        pltpu.VMEM((2, NX, TOK, CG), F32),
         pltpu.VMEM((2, NX, TOK, CG), BF16),
         pltpu.VMEM((2, NX, TOK, CG), BF16),
         pltpu.VMEM((2, NX, TOK, CG), BF16),
         pltpu.VMEM((2, NX, TOK, CG), BF16),
         pltpu.SemaphoreType.DMA((2, 3, NK)),
         pltpu.SemaphoreType.DMA((2, 3, NK)),
+        pltpu.SemaphoreType.DMA((7,)),
         pltpu.SemaphoreType.DMA((2, NX)),
         pltpu.SemaphoreType.DMA((2, 2, NX)),
-        pltpu.SemaphoreType.DMA((2, 6)),
+        pltpu.SemaphoreType.DMA((2, 9)),
         pltpu.SemaphoreType.DMA((4, 2)),
         pltpu.SemaphoreType.DMA((2, 2, NX)),
         pltpu.SemaphoreType.DMA((2, 2, NX)),
@@ -676,16 +724,16 @@
             jax.ShapeDtypeStruct((TOK, CG), BF16),
             jax.ShapeDtypeStruct((8, LANES), F32),
         ),
-        in_specs=[pl.BlockSpec(memory_space=pl.ANY)] * 2 + [vmem] * 4,
+        in_specs=[pl.BlockSpec(memory_space=pltpu.HBM)] * 9,
         out_specs=(vmem,) * 3,
         scratch_shapes=scratch,
         compiler_params=pltpu.CompilerParams(
-            collective_id=0, has_side_effects=True, vmem_limit_bytes=48 * 2**20
+            collective_id=0, has_side_effects=True, vmem_limit_bytes=63 * 2**20
         ),
         cost_estimate=pl.CostEstimate(
             flops=2 * 6 * TOK * CG * 4096, bytes_accessed=2**22, transcendentals=2**17
         ),
-    )(features, grad_out, w_value, w_query, w_out.T, prm)
+    )(features, grad_out, w_value, w_query, w_out.T, decays, freqs, residues, skips.reshape(1, CG))
     return mixed, grad_in, res[0].reshape(CB, ORDER).T
 
 

time: 123 us -> 116 us (0.943)
  local copies, waits for them, and re-layouts: 7.6 us -> 3.63 us
  Pallas kernels: 115 us -> 112 us
    pallas_call x1, Pallas kernels: 115 us -> 112 us  [body(): pl.pallas_call(kernel, out_shape=(jax.ShapeDtypeStruct((TOK, CG), BF16),...]
    unnamed x14 -> x4, local copies, waits for them, and re-layouts: 4.61 us -> 2.26 us
where the time goes in v4:
time: 116 us
  Pallas kernels  112 us (97%)
  local copies, waits for them, and re-layouts  3.63 us (3%)
    pallas_call x1, Pallas kernels, body(): pl.pallas_call(kernel, out_shape=(jax.ShapeDtypeStruct((TOK, CG), BF16),...  112 us

profile of v4, /device:TPU:1, one launch (start us, length us, event | category | flops | bytes accessed | tf_op | source)
XLA Modules:
  0.0 115.8 jit_solution(14433729516266142868)
XLA Ops:
  0.6 111.6 %shard_map.112 = (bf16[128,512]{1,0:T(8,128)(2,1)}, bf16[128,512]{1,0:T(8,128)(2,1)}, f32[8,128]{1,0:T(8,128)}) custom-call(bf16[128,4096]{1,0:T(8,128)(2,1)} %f_ref.1, bf16[128,4096]{1,0:T(8,128)(2,1)} %g_ref.1, bf16[64,512]{1,0:T(8,128)(2,1)} %wv_ref.1, bf16[64,512]{1,0:T(8,128)(2,1)} %wq_ref.1, bf16[64,512]{1,0:T(8,128)(2,1)} %bitcast.4, ...), custom_call_target="tpu_custom_call" | custom-call | flops 3221225472 | bytes 4194304 | tf_op jit(solution)/shard_map/pallas_call | solution.py:720
  112.2 0.7 slice_reduce_fusion
  112.9 0.7 reshape_squeeze.3
  113.6 0.0 copy-start
  113.6 1.6 %copy.14 = bf16[128,512]{1,0:T(8,128)(2,1)} copy(bf16[128,512]{1,0:T(8,128)(2,1)} %get-tuple-element.12) | data formatting | bytes 262144
  115.2 0.0 copy-done
  115.2 0.7 copy.15
Async XLA Ops:
  113.6 1.6 %copy-start = (bf16[128,512]{1,0:T(8,128)(2,1)S(1)}, bf16[128,512]{1,0:T(8,128)(2,1)}, u32[]{:S(2)}) copy-start(bf16[128,512]{1,0:T(8,128)(2,1)} %get-tuple-element.13) | copy-start | bytes 393220

commit v5 on v4

--- a/solution.py
+++ b/solution.py
@@ -638,11 +638,11 @@
     exchange(3)
     shared(1)
     lax.fori_loop(0, NX, early, 0)
-    amplitudes(x32, gs, f, states, bas, res_ref)
     exchanged(3)
     put(2, from_chunks(3))
     shared(2)
     scatter(1, lambda k, b: pre[k, b] + dot(gat[2, halves[k], :], w[0, b].reshape(CG, CG), NT))
+    amplitudes(x32, gs, f, states, bas, res_ref)
     collect(0, mixed_ref)
     collect(1, gin_ref)
 

time: 116 us -> 116 us (level)
  no operation moved by 1% of the time
where the time goes in v5:
time: 116 us
  Pallas kernels  112 us (97%)
  local copies, waits for them, and re-layouts  3.63 us (3%)
    pallas_call x1, Pallas kernels, body(): pl.pallas_call(kernel, out_shape=(jax.ShapeDtypeStruct((TOK, CG), BF16),...  112 us

profile of v5, /device:TPU:1, one launch (start us, length us, event | category | flops | bytes accessed | tf_op | source)
XLA Modules:
  0.0 115.8 jit_solution(6612106526820572085)
XLA Ops:
  0.6 111.6 %shard_map.112 = (bf16[128,512]{1,0:T(8,128)(2,1)}, bf16[128,512]{1,0:T(8,128)(2,1)}, f32[8,128]{1,0:T(8,128)}) custom-call(bf16[128,4096]{1,0:T(8,128)(2,1)} %f_ref.1, bf16[128,4096]{1,0:T(8,128)(2,1)} %g_ref.1, bf16[64,512]{1,0:T(8,128)(2,1)} %wv_ref.1, bf16[64,512]{1,0:T(8,128)(2,1)} %wq_ref.1, bf16[64,512]{1,0:T(8,128)(2,1)} %bitcast.4, ...), custom_call_target="tpu_custom_call" | custom-call | flops 3221225472 | bytes 4194304 | tf_op jit(solution)/shard_map/pallas_call | solution.py:720
  112.2 0.7 slice_reduce_fusion
  112.9 0.7 reshape_squeeze.3
  113.6 0.0 copy-start
  113.6 1.6 %copy.14 = bf16[128,512]{1,0:T(8,128)(2,1)} copy(bf16[128,512]{1,0:T(8,128)(2,1)} %get-tuple-element.12) | data formatting | bytes 262144
  115.2 0.0 copy-done
  115.2 0.7 copy.15
Async XLA Ops:
  113.6 1.6 %copy-start = (bf16[128,512]{1,0:T(8,128)(2,1)S(1)}, bf16[128,512]{1,0:T(8,128)(2,1)}, u32[]{:S(2)}) copy-start(bf16[128,512]{1,0:T(8,128)(2,1)} %get-tuple-element.13) | copy-start | bytes 393220
